TPU v7x, 32 devices: a whole 2x2x4 slice. The times are simulated.
32 devices in a mesh: angle: 2 (over x), gx: 8 (over z, y), gy: 2 (over core).
Axes of the slice: x: 2, y: 2, z: 4, core: 2. Of those that a mesh axis runs over, the one named last changes fastest.
Arguments:
- electric: float32 [4, 3, 32, 64, 256], P('angle', None, 'gx', 'gy'), parts along dimension 0, may hold values from -3 to 3
- magnetic: float32 [4, 3, 32, 64, 256], P('angle', None, 'gx', 'gy'), parts along dimension 0, may hold values from -3 to 3
- polarize: float32 [4, 3, 32, 64, 256], P('angle', None, 'gx', 'gy'), parts along dimension 0, may hold values from -1.5 to 1.5
- currents: float32 [4, 3, 32, 64, 256], P('angle', None, 'gx', 'gy'), parts along dimension 0, may hold values from -1.5 to 1.5
- material: int32 [32, 64, 256], P('gx', 'gy'), may hold values from 0 to 7
- pole_of: int32 [8], replicated, may hold values from 0 to 3
- eps_inf: float32 [8], replicated, may hold values from 1 to 1.2
- pole_decay: float32 [4], replicated, may hold values from 0.5 to 0.95
- pole_freq: float32 [4], replicated, may hold values from 0.05 to 0.2
- pole_strength: float32 [4], replicated, may hold values from 0.3 to 2
- bloch: float32 [4], P('angle'), parts along dimension 0, may hold values from -3.140625 to 3.140625
Outputs:
- electric_out: float32 [4, 3, 32, 64, 256], P('angle', None, 'gx', 'gy'), parts along dimension 0
- magnetic_out: float32 [4, 3, 32, 64, 256], P('angle', None, 'gx', 'gy'), parts along dimension 0
- polar_out: float32 [4, 3, 32, 64, 256], P('angle', None, 'gx', 'gy'), parts along dimension 0
- current_out: float32 [4, 3, 32, 64, 256], P('angle', None, 'gx', 'gy'), parts along dimension 0
- harmonics: float32 [4, 8, 8, 32], P('angle', None, None, 'gx'), parts along dimension 0
There are 2 independent parts, one for each index of `angle`. A program takes and returns all parts, laid end to end along the dimension named above; an argument that names none is the same for every part. Nothing has to cross between parts.
All inputs are finite; a program needn't handle non-finite values.
Results may differ from a plain program's by a relative error of at most 0.0003.
Values sent between devices are 32-bit elements; how exact they have to be, the bound alone decides.
No kernel may reach another device: no remote copies, remote signals or barrier semaphores. Data moves between devices by JAX's collectives and lax.ppermute only.
A program may use at most 128 MiB of HBM per device.

v0:
```python
import functools
import math

import jax
import jax.numpy as jnp
import numpy as np
from jax import lax
from jax.experimental import pallas as pl
from jax.experimental.pallas import tpu as pltpu
from jax.sharding import PartitionSpec as P

STEPS = 8
HARM = 8
EDGE = 8
courant = 0.5
VMEM_LIMIT = 24 << 20


def next_y(v):
    return pltpu.roll(v, v.shape[0] - 1, 0)


def prev_y(v):
    return pltpu.roll(v, 1, 0)


def next_z(v):
    lane = lax.broadcasted_iota(jnp.int32, v.shape, 1)
    return jnp.where(lane == v.shape[1] - 1, 0.0, pltpu.roll(v, v.shape[1] - 1, 1))


def prev_z(v):
    lane = lax.broadcasted_iota(jnp.int32, v.shape, 1)
    return jnp.where(lane == 0, 0.0, pltpu.roll(v, 1, 1))


def turn(pair, cos_v, sin_v):
    return cos_v * pair[0] - sin_v * pair[1], sin_v * pair[0] + cos_v * pair[1]


def sublane(v):
    return lax.broadcasted_iota(jnp.int32, v.shape, 0)


def weave(first, second):
    row = sublane(first)
    return jnp.where((row < 2) | (row >= 6), first, pltpu.roll(second, 4, 0))


def edge_rows(ref, at, rows):
    low = ref[at + (slice(0, 8),)]
    high = ref[at + (slice(rows - 8, rows),)]
    return jnp.where(sublane(low) < 4, low, high)


def pack_edges(fields, out, rows):
    e, h, p, j = fields
    parts, comps, planes = e.shape[:3]
    for r in range(parts):
        for g, (one, two) in enumerate(((e, h), (p, j))):
            for k in range(comps):
                for x in range(planes):
                    at = (r, k, x)
                    tile = weave(edge_rows(one, at, rows), edge_rows(two, at, rows))
                    out[((r * 2 + g) * comps + k) * planes + x] = tile


def unpack_edges(recv, fields, phase, rows):
    e, h, p, j = fields
    comps, planes = e.shape[1:3]
    depth = e.shape[4]
    row = lax.broadcasted_iota(jnp.int32, (8, depth), 0)
    cos_v = jnp.where(row < 4, phase[4], phase[6])
    sin_v = jnp.where(row < 4, phase[5], phase[7])
    for g, (one, two) in enumerate(((e, h), (p, j))):
        for k in range(comps):
            for x in range(planes):
                pair = [recv[((r * 2 + g) * comps + k) * planes + x] for r in range(2)]
                for dst in (one, two):
                    re, im = turn(pair, cos_v, sin_v)
                    dst[0, k, x, rows:] = re
                    dst[1, k, x, rows:] = im
                    pair = [pltpu.roll(v, 4, 0) for v in pair]


def curl_e_x(ey, ez):
    return (next_y(ez) - ez) - (next_z(ey) - ey)


def magnetic_full(e, h, r, x, nxt):
    ex, ey, ez = (e[r, k, x] for k in range(3))
    ny_, nz_ = nxt
    h[r, 0, x] = h[r, 0, x] - courant * curl_e_x(ey, ez)
    h[r, 1, x] = h[r, 1, x] - courant * ((next_z(ex) - ex) - (nz_ - ez))
    h[r, 2, x] = h[r, 2, x] - courant * ((ny_ - ey) - (next_y(ex) - ex))


def magnetic_open(ex, ey, ez, hy, hz):
    hy = hy - courant * ((next_z(ex) - ex) + ez)
    hz = hz - courant * ((0.0 - ey) - (next_y(ex) - ex))
    return hy, hz


def polarize_step(e, p, j, coef, r, x):
    for k in range(3):
        now = coef[1, x] * j[r, k, x] + coef[2, x] * (coef[3, x] * e[r, k, x] - p[r, k, x])
        j[r, k, x] = now
        p[r, k, x] = p[r, k, x] + courant * now


def electric_step(e, h, j, coef, r, x, prev):
    hx, hy, hz = (h[r, k, x] for k in range(3))
    inv = coef[0, x]
    e[r, 0, x] = e[r, 0, x] + inv * ((hz - prev_y(hz)) - (hy - prev_z(hy)) - j[r, 0, x])
    dz, dy = hz, hy
    if prev is not None:
        dz, dy = hz - prev[1], hy - prev[0]
    e[r, 1, x] = e[r, 1, x] + inv * ((hx - prev_z(hx)) - dz - j[r, 1, x])
    e[r, 2, x] = e[r, 2, x] + inv * (dy - (hx - prev_y(hx)) - j[r, 2, x])


def response(inv, dhy, dhz):
    dex = inv * ((dhz - prev_y(dhz)) - (dhy - prev_z(dhy)))
    return dex, 0.0 - inv * dhz, inv * dhy


def note_top(e, rec, r, x, step, rows):
    depth = e.shape[4]
    top = e[r, 0, x, 0:rows, depth - 128 :]
    lane = lax.broadcasted_iota(jnp.int32, top.shape, 1)
    rec[r, x] = jnp.where(lane == step, pltpu.roll(top, (step + 1) % 128, 1), rec[r, x])


def start_body(rows, e_in, h_in, p_in, j_in, mat, e, h, p, j, edges):
    for src, dst in ((e_in, e), (h_in, h), (p_in, p), (j_in, j)):
        dst[:, :, :, 0:rows] = src[...]
        dst[:, :, :, rows:] = jnp.zeros(dst.shape[:3] + (EDGE, dst.shape[4]), jnp.float32)
    pack_edges((e_in, h_in, p_in, j_in), edges, rows)
    base = 2 * 2 * 3 * e_in.shape[2]
    for x in range(e_in.shape[2]):
        edges[base + x] = edge_rows(mat, (x,), rows).astype(jnp.float32)


def cell_tables(kind, pole_of, eps, dec, frq, stg):
    vals = [jnp.full(kind.shape, t, jnp.float32) for t in (eps[0], dec[pole_of[0]], frq[pole_of[0]], stg[pole_of[0]])]
    for m in range(1, eps.shape[0]):
        hit = kind == m
        pole = pole_of[m]
        for i, t in enumerate((eps[m], dec[pole], frq[pole], stg[pole])):
            vals[i] = jnp.where(hit, t, vals[i])
    vals[0] = courant / vals[0]
    return vals


def coef_body(rows, mat, pole_of, eps, dec, frq, stg, coef):
    for x in range(mat.shape[0]):
        for y in range(0, rows, 8):
            vals = cell_tables(mat[x, y : y + 8], pole_of, eps, dec, frq, stg)
            for i in range(4):
                coef[i, x, y : y + 8] = vals[i]
        for i in range(4):
            coef[i, x, rows:] = jnp.zeros((EDGE, coef.shape[3]), jnp.float32)


def send_body(rows, first, refs):
    refs = list(refs)
    phase, par, edges = refs[0:3]
    refs = refs[3:]
    if first:
        pole_of, eps, dec, frq, stg = refs[0:5]
        refs = refs[5:]
    e, h, p, j, coef, e0, ev, od, msg = refs[5:]
    planes = e.shape[2]
    last = planes - 1
    unpack_edges(edges, (e, h, p, j), phase, rows)
    if first:
        base = 2 * 2 * 3 * planes
        for x in range(planes):
            kind = edges[base + x].astype(jnp.int32)
            vals = cell_tables(kind, pole_of, eps, dec, frq, stg)
            for i in range(4):
                coef[i, x, rows:] = vals[i]
    up, dn = par[0], 1 - par[0]
    half = 4 * rows
    for r in range(2):
        tiles_d, tiles_u = [], []
        magnetic_full(e, h, r, 0, (e[r, 1, 1], e[r, 2, 1]))
        magnetic_full(e, h, r, last - 1, (e[r, 1, last], e[r, 2, last]))
        ex, ey, ez = (e[r, k, last] for k in range(3))
        h[r, 0, last] = h[r, 0, last] - courant * curl_e_x(ey, ez)
        hs = magnetic_open(ex, ey, ez, h[r, 1, last], h[r, 2, last])
        for k in range(2):
            h[r, 1 + k, last] = hs[k]
            msg[up, (2 * r + k) * rows : (2 * r + k + 1) * rows] = hs[k][0:rows]
            tiles_u.append(hs[k][rows:])
            now = e[r, 1 + k, 0]
            e0[r, k] = now
            msg[dn, (2 * r + k) * rows : (2 * r + k + 1) * rows] = now[0:rows]
            tiles_d.append(now[rows:])
        polarize_step(e, p, j, coef, r, 0)
        polarize_step(e, p, j, coef, r, last)
        electric_step(e, h, j, coef, r, 0, None)
        electric_step(e, h, j, coef, r, last, (h[r, 1, last - 1], h[r, 2, last - 1]))
        ex, ey, ez = (e[r, k, last] for k in range(3))
        hs = magnetic_open(ex, ey, ez, h[r, 1, last], h[r, 2, last])
        for k in range(2):
            at = half + (2 * r + k) * rows
            msg[up, at : at + rows] = hs[k][0:rows]
            now = e[r, 1 + k, 0]
            msg[dn, at : at + rows] = now[0:rows]
            row = sublane(tiles_d[k])
            tiles_d[k] = jnp.where(row == 1, pltpu.roll(now[rows:], 2, 0), tiles_d[k])
        at = 2 * half + 8 * r
        msg[up, at : at + 8] = weave(*tiles_u)
        msg[dn, at : at + 8] = weave(*tiles_d)
    if first:
        at = 2 * half + 16
        msg[up, at : at + rows + EDGE] = coef[0, last]
        msg[dn, at : at + rows + EDGE] = coef[0, 0]
    ev[...] = msg[0]
    od[...] = msg[1]


def inner_body(rows, step, refs):
    e, h, p, j, coef, rec = refs[6:]
    planes = e.shape[2]
    for r in range(2):
        for x in range(1, planes - 2):
            magnetic_full(e, h, r, x, (e[r, 1, x + 1], e[r, 2, x + 1]))
        for x in range(1, planes - 1):
            polarize_step(e, p, j, coef, r, x)
            electric_step(e, h, j, coef, r, x, (h[r, 1, x - 1], h[r, 2, x - 1]))
        for x in range(planes - 1):
            note_top(e, rec, r, x, step, rows)
        for x in range(1, planes - 2):
            magnetic_full(e, h, r, x, (e[r, 1, x + 1], e[r, 2, x + 1]))
        for x in range(1, planes - 1):
            polarize_step(e, p, j, coef, r, x)


def finish_body(rows, step, first, final, refs):
    refs = list(refs)
    phase, par, ev, od, e0 = refs[0:5]
    refs = refs[5:]
    if not first:
        far_in = refs[0]
        refs = refs[1:]
    refs = refs[6:]
    e, h, p, j, rec = refs[0:5]
    coef = refs[5]
    refs = refs[6:]
    if first:
        far = refs[0]
        refs = refs[1:]
    else:
        far = far_in
    if final:
        e_out, h_out, p_out, j_out, wave, harm = refs[0:6]
        refs = refs[6:]
    else:
        edges = refs[0]
        refs = refs[1:]
    msg, = refs
    planes = e.shape[2]
    last = planes - 1
    half = 4 * rows
    msg[0] = ev[...]
    msg[1] = od[...]
    fa, fb = par[0], 1 - par[0]
    if first:
        far[0] = msg[fb, 2 * half + 16 : 2 * half + 16 + rows + EDGE]
        far[1] = msg[fa, 2 * half + 16 : 2 * half + 16 + rows + EDGE]
    inv_lo, inv_hi = far[0], far[1]

    def arrived(side, cos_v, sin_v):
        res = []
        for k in range(2):
            raw = []
            for r in range(2):
                tile = msg[side, 2 * half + 8 * r : 2 * half + 8 * r + 8]
                if k == 1:
                    tile = pltpu.roll(tile, 4, 0)
                at = (2 * r + k) * rows
                one = jnp.concatenate([msg[side, at : at + rows], tile], axis=0)
                two = jnp.concatenate([msg[side, half + at : half + at + rows], pltpu.roll(tile, 6, 0)], axis=0)
                raw.append((one, two))
            res.append((turn((raw[0][0], raw[1][0]), cos_v, sin_v), turn((raw[0][1], raw[1][1]), cos_v, sin_v)))
        return res

    above = arrived(fa, phase[0], phase[1])
    for r in range(2):
        a0y, a0z = above[0][0][r], above[1][0][r]
        dhy, dhz = courant * a0z, 0.0 - courant * a0y
        hy = h[r, 1, last] + dhy
        hz = h[r, 2, last] + dhz
        h[r, 1, last] = hy
        h[r, 2, last] = hz
        for k, d in enumerate(response(coef[0, last], dhy, dhz)):
            e[r, k, last] = e[r, k, last] + d
        note_top(e, rec, r, last, step, rows)
        a1y = above[0][1][r] + inv_hi * hz
        a1z = above[1][1][r] - inv_hi * hy
        magnetic_full(e, h, r, last - 1, (e[r, 1, last], e[r, 2, last]))
        magnetic_full(e, h, r, last, (a1y, a1z))
        polarize_step(e, p, j, coef, r, last)
    below = arrived(fb, phase[2], phase[3])
    for r in range(2):
        dhy, dhz = courant * e0[r, 1], 0.0 - courant * e0[r, 0]
        e[r, 1, 0] = e[r, 1, 0] + coef[0, 0] * (below[1][0][r] + dhz)
        e[r, 2, 0] = e[r, 2, 0] - coef[0, 0] * (below[0][0][r] + dhy)
        dex, dey, dez = response(inv_lo, dhy, dhz)
        hy, hz = magnetic_open(dex, dey, dez, dhy, dhz)
        b1y = below[0][1][r] + hy + courant * e[r, 2, 0]
        b1z = below[1][1][r] + hz - courant * e[r, 1, 0]
        magnetic_full(e, h, r, 0, (e[r, 1, 1], e[r, 2, 1]))
        polarize_step(e, p, j, coef, r, 0)
        electric_step(e, h, j, coef, r, 0, (b1y, b1z))
        for x in range(1, planes):
            electric_step(e, h, j, coef, r, x, (h[r, 1, x - 1], h[r, 2, x - 1]))
        for x in range(planes):
            note_top(e, rec, r, x, step + 1, rows)
    if not final:
        pack_edges((e, h, p, j), edges, rows)
        return
    for src, dst in ((e, e_out), (h, h_out), (p, p_out), (j, j_out)):
        dst[...] = src[:, :, :, 0:rows]
    for x in range(planes):
        re, im = (
            jnp.dot(wave[...], rec[r, x], precision=lax.Precision.HIGHEST, preferred_element_type=jnp.float32)
            for r in range(2)
        )
        harm[0, x] = re[0:HARM] + im[HARM:]
        harm[1, x] = im[0:HARM] - re[HARM:]


def call(body, ins, outs, aliases=None, smem=(), scratch=()):
    shapes = [jax.ShapeDtypeStruct(s, d) for s, d in outs]
    vm = pl.BlockSpec(memory_space=pltpu.VMEM)
    sm = pl.BlockSpec(memory_space=pltpu.SMEM)
    return pl.pallas_call(
        body,
        out_shape=shapes,
        in_specs=[sm if i in smem else vm for i in range(len(ins))],
        out_specs=[vm] * len(outs),
        input_output_aliases=aliases or {},
        scratch_shapes=list(scratch),
        compiler_params=pltpu.CompilerParams(vmem_limit_bytes=VMEM_LIMIT),
    )(*ins)


def swap(block, axis, shift):
    count = lax.axis_size(axis)
    pairs = [(i % count, (i + 1) % count) for i in range(shift, count, 2)]
    return lax.ppermute(block, axis, [q for a, b in pairs for q in ((a, b), (b, a))])


def per_device(
    electric, magnetic, polarize, currents, material, pole_of, eps_inf, pole_decay, pole_freq, pole_strength, bloch
):
    parts, comps, planes, rows, depth = electric.shape
    count_x, count_y = lax.axis_size("gx"), lax.axis_size("gy")
    assert count_x % 2 == 0 and count_y == 2 and planes >= 4
    where_x, where_y = lax.axis_index("gx"), lax.axis_index("gy")
    width_y = rows * count_y
    f32 = jnp.float32
    ext = (rows + EDGE, depth)
    cos_b, sin_b = jnp.cos(bloch), jnp.sin(bloch)

    def hop(at, edge, axis, sign):
        return [jnp.where(at == edge, cos_b[axis], 1.0), jnp.where(at == edge, sign * sin_b[axis], 0.0)]

    phase = jnp.stack(
        hop(where_x, count_x - 1, 0, 1.0)
        + hop(where_x, 0, 0, -1.0)
        + hop(where_y, count_y - 1, 1, 1.0)
        + hop(where_y, 0, 1, -1.0)
    )
    par = jnp.reshape(where_x % 2, (1,)).astype(jnp.int32)
    angle = 2.0 * math.pi / width_y * (np.arange(HARM)[:, None] * np.arange(width_y)[None, :] % width_y)
    waves = np.concatenate([np.cos(angle), np.sin(angle)]) / math.sqrt(width_y)
    waves = np.stack(np.split(waves, count_y, axis=1)).astype(np.float32)
    wave = lax.dynamic_index_in_dim(jnp.asarray(waves), where_y, 0, keepdims=False)

    state_shape = ((parts, comps, planes) + ext, f32)
    coef_shape = ((4, planes) + ext, f32)
    tiles = 2 * 2 * comps * planes
    e, h, p, j, edges = call(
        functools.partial(start_body, rows),
        (electric, magnetic, polarize, currents, material),
        [state_shape] * 4 + [((tiles + planes, 8, depth), f32)],
    )
    tables = (pole_of, eps_inf, pole_decay, pole_freq, pole_strength)
    (coef,) = call(
        functools.partial(coef_body, rows), (material,) + tables, [coef_shape], smem=range(1, 6)
    )
    rec = jnp.zeros((2, planes, rows, 128), f32)
    far = None
    for step in range(0, STEPS, 2):
        first, final = step == 0, step == STEPS - 2
        edges = swap(edges, "gy", 0)
        size = 8 * rows + 16 + (rows + EDGE if first else 0)
        extra = tables if first else ()
        ins = (phase, par, edges) + extra + (e, h, p, j, coef)
        n = 3 + len(extra)
        e, h, p, j, coef, e0, ev, od = call(
            lambda *refs, first=first: send_body(rows, first, refs),
            ins,
            [state_shape] * 4 + [coef_shape, ((2, 2) + ext, f32)] + [((size, depth), f32)] * 2,
            {n + i: i for i in range(5)},
            smem=(0, 1) + tuple(range(3, n)),
            scratch=[pltpu.VMEM((2, size, depth), f32)],
        )
        ev, od = swap(ev, "gx", 0), swap(od, "gx", 1)
        e, h, p, j, coef, rec = call(
            lambda *refs, step=step: inner_body(rows, step, refs),
            (e, h, p, j, coef, rec),
            [state_shape] * 4 + [coef_shape, (rec.shape, f32)],
            {i: i for i in range(6)},
        )
        ins = (phase, par, ev, od, e0) + (() if first else (far,))
        n = len(ins)
        ins = ins + (e, h, p, j, rec, coef)
        outs = [state_shape] * 4 + [(rec.shape, f32), coef_shape]
        if first:
            outs.append(((2,) + ext, f32))
        if final:
            ins = ins + (wave,)
            outs += [(electric.shape, f32)] * 4 + [((2, planes, HARM, 128), f32)]
        else:
            outs.append(((tiles, 8, depth), f32))

        def body(*refs, first=first, final=final, step=step, n=n):
            refs = list(refs)
            if final:
                w = refs.pop(n + 6)
                refs.insert(len(refs) - 2, w)
            finish_body(rows, step, first, final, refs)

        res = call(
            body, ins, outs, {n + i: i for i in range(6)}, smem=(0, 1), scratch=[pltpu.VMEM((2, size, depth), f32)]
        )
        e, h, p, j, rec, coef = res[0:6]
        res = res[6:]
        if first:
            far = res[0]
            res = res[1:]
        if not final:
            edges = res[0]
    *fields, harm = res
    harm = harm + swap(harm, "gy", 0)
    history = jnp.transpose(harm[..., :STEPS], (0, 3, 2, 1))
    return (*fields, history)


def solution(mesh):
    field = P("angle", None, "gx", "gy", None)
    in_specs = (field,) * 4 + (P("gx", "gy", None),) + (P(),) * 5 + (P("angle"),)
    out_specs = (field,) * 4 + (P("angle", None, None, "gx"),)
    return jax.shard_map(per_device, mesh=mesh, in_specs=in_specs, out_specs=out_specs, check_vma=False)
```

profile of v0, /device:TPU:1, one launch (start us, length us, event | category | flops | bytes accessed | tf_op | source)
XLA Modules:
  0.0 106.3 jit_solution(8514446283249845736)
XLA Ops:
  19.4 1.3 %shard_map.157 = (f32[2,3,4,40,256]{4,3,2,1,0:T(8,128)S(1)}, f32[2,3,4,40,256]{4,3,2,1,0:T(8,128)S(1)}, f32[2,3,4,40,256]{4,3,2,1,0:T(8,128)S(1)}, f32[2,3,4,40,...) custom-call(f32[8]{0:T(128)S(1)} %stack.35.refs_0_, ...), custom_call_target="tpu_custom_call", output_to_operand_aliasing={{0}: (8, {}), {1}: (9, {}), {2}: (10, {}), {3}: (11, {}), {... | custom-call | tf_op jit(solution)/shard_map/pallas_call | solution.py:340
  21.6 2.7 %collective-permute-start.1 = (f32[312,256]{1,0:T(8,128)S(1)}, f32[312,256]{1,0:T(8,128)S(1)}, u32[]{:S(2)}, u32[]{:S(2)}) collective-permute-start(f32[312,256]{1,0:T(8,128)S(1)} %get-tuple-element.98), channel_id=1, source_target_pairs={{0,2},{2,0},{4,6},{6,4},{8,10},{10,8},{12,14},{14,12},{1,3},{3,1},... | collective-permute-start | bytes 958472 | tf_op jit(solution)/shard_map/ppermute | solution.py:354
  24.3 3.3 %collective-permute-start.2 = (f32[312,256]{1,0:T(8,128)S(1)}, f32[312,256]{1,0:T(8,128)S(1)}, u32[]{:S(2)}, u32[]{:S(2)}) collective-permute-start(f32[312,256]{1,0:T(8,128)S(1)} %get-tuple-element.99), channel_id=1, source_target_pairs={{2,4},{4,2},{6,8},{8,6},{10,12},{12,10},{14,0},{0,14},{3,5},{5,3},... | collective-permute-start | bytes 958472 | tf_op jit(solution)/shard_map/ppermute | solution.py:354
  29.2 9.8 %collective-permute-done.1.refs_2_ = f32[312,256]{1,0:T(8,128)S(1)} collective-permute-done((f32[312,256]{1,0:T(8,128)S(1)}, f32[312,256]{1,0:T(8,128)S(1)}, u32[]{:S(2)}, u32[]{:S(2)}) %collective-permute-start.1) | collective-permute-done | bytes 319520 | tf_op jit(solution)/shard_map/ppermute | solution.py:354
  39.0 1.6 %shard_map.159 = (f32[2,3,4,40,256]{4,3,2,1,0:T(8,128)S(1)}, f32[2,3,4,40,256]{4,3,2,1,0:T(8,128)S(1)}, f32[2,3,4,40,256]{4,3,2,1,0:T(8,128)S(1)}, f32[2,3,4,40,...) custom-call(f32[8]{0:T(128)S(1)} %stack.35.refs_0_, ...), custom_call_target="tpu_custom_call", output_to_operand_aliasing={{0}: (5, {}), {1}: (6, {}), {2}: (7, {}), {3}: (8, {}), {4}... | custom-call | tf_op jit(solution)/shard_map/pallas_call | solution.py:340
  41.3 1.3 %collective-permute-done.3.refs_2_ = f32[48,8,256]{2,1,0:T(8,128)S(1)} collective-permute-done((f32[48,8,256]{2,1,0:T(8,128)S(1)}, f32[48,8,256]{2,1,0:T(8,128)S(1)}, u32[]{:S(2)}, u32[]{:S(2)}) %collective-permute-start.3) | collective-permute-done | bytes 393248 | tf_op jit(solution)/shard_map/ppermute | solution.py:354
  43.9 1.5 %collective-permute-start.4 = (f32[272,256]{1,0:T(8,128)S(1)}, f32[272,256]{1,0:T(8,128)S(1)}, u32[]{:S(2)}, u32[]{:S(2)}) collective-permute-start(f32[272,256]{1,0:T(8,128)S(1)} %get-tuple-element.118), channel_id=1, source_target_pairs={{0,2},{2,0},{4,6},{6,4},{8,10},{10,8},{12,14},{14,12},{1,3},{3,1},... | collective-permute-start | bytes 835592 | tf_op jit(solution)/shard_map/ppermute | solution.py:354
  45.4 3.3 %collective-permute-start.5 = (f32[272,256]{1,0:T(8,128)S(1)}, f32[272,256]{1,0:T(8,128)S(1)}, u32[]{:S(2)}, u32[]{:S(2)}) collective-permute-start(f32[272,256]{1,0:T(8,128)S(1)} %get-tuple-element.119), channel_id=1, source_target_pairs={{2,4},{4,2},{6,8},{8,6},{10,12},{12,10},{14,0},{0,14},{3,5},{5,3},... | collective-permute-start | bytes 835592 | tf_op jit(solution)/shard_map/ppermute | solution.py:354
  49.2 8.6 %collective-permute-done.4.refs_2_ = f32[272,256]{1,0:T(8,128)S(1)} collective-permute-done((f32[272,256]{1,0:T(8,128)S(1)}, f32[272,256]{1,0:T(8,128)S(1)}, u32[]{:S(2)}, u32[]{:S(2)}) %collective-permute-start.4) | collective-permute-done | bytes 278560 | tf_op jit(solution)/shard_map/ppermute | solution.py:354
  57.8 1.6 %shard_map.162 = (f32[2,3,4,40,256]{4,3,2,1,0:T(8,128)S(1)}, f32[2,3,4,40,256]{4,3,2,1,0:T(8,128)S(1)}, f32[2,3,4,40,256]{4,3,2,1,0:T(8,128)S(1)}, f32[2,3,4,40,...) custom-call(f32[8]{0:T(128)S(1)} %stack.35.refs_0_, ...), custom_call_target="tpu_custom_call", output_to_operand_aliasing={{0}: (6, {}), {1}: (7, {}), {2}: (8, {}), {3}: (9, {}), {4}... | custom-call | tf_op jit(solution)/shard_map/pallas_call | solution.py:340
  59.4 1.3 %collective-permute-start.6 = (f32[48,8,256]{2,1,0:T(8,128)S(1)}, f32[48,8,256]{2,1,0:T(8,128)S(1)}, u32[]{:S(2)}, u32[]{:S(2)}) collective-permute-start(f32[48,8,256]{2,1,0:T(8,128)S(1)} %get-tuple-element.134), channel_id=1, source_target_pairs={{0,1},{1,0},{2,3},{3,2},{4,5},{5,4},{6,7},{7,6},{8,9},{9,8},{10,11... | collective-permute-start | bytes 1179656 | tf_op jit(solution)/shard_map/ppermute | solution.py:354
  60.7 1.3 %collective-permute-done.6.refs_2_ = f32[48,8,256]{2,1,0:T(8,128)S(1)} collective-permute-done((f32[48,8,256]{2,1,0:T(8,128)S(1)}, f32[48,8,256]{2,1,0:T(8,128)S(1)}, u32[]{:S(2)}, u32[]{:S(2)}) %collective-permute-start.6) | collective-permute-done | bytes 393248 | tf_op jit(solution)/shard_map/ppermute | solution.py:354
  63.2 1.5 %collective-permute-start.7 = (f32[272,256]{1,0:T(8,128)S(1)}, f32[272,256]{1,0:T(8,128)S(1)}, u32[]{:S(2)}, u32[]{:S(2)}) collective-permute-start(f32[272,256]{1,0:T(8,128)S(1)} %get-tuple-element.140), channel_id=1, source_target_pairs={{0,2},{2,0},{4,6},{6,4},{8,10},{10,8},{12,14},{14,12},{1,3},{3,1},... | collective-permute-start | bytes 835592 | tf_op jit(solution)/shard_map/ppermute | solution.py:354
  64.7 3.3 %collective-permute-start.8 = (f32[272,256]{1,0:T(8,128)S(1)}, f32[272,256]{1,0:T(8,128)S(1)}, u32[]{:S(2)}, u32[]{:S(2)}) collective-permute-start(f32[272,256]{1,0:T(8,128)S(1)} %get-tuple-element.141), channel_id=1, source_target_pairs={{2,4},{4,2},{6,8},{8,6},{10,12},{12,10},{14,0},{0,14},{3,5},{5,3},... | collective-permute-start | bytes 835592 | tf_op jit(solution)/shard_map/ppermute | solution.py:354
  68.5 8.6 %collective-permute-done.7.refs_2_ = f32[272,256]{1,0:T(8,128)S(1)} collective-permute-done((f32[272,256]{1,0:T(8,128)S(1)}, f32[272,256]{1,0:T(8,128)S(1)}, u32[]{:S(2)}, u32[]{:S(2)}) %collective-permute-start.7) | collective-permute-done | bytes 278560 | tf_op jit(solution)/shard_map/ppermute | solution.py:354
  77.1 1.6 %shard_map.165 = (f32[2,3,4,40,256]{4,3,2,1,0:T(8,128)S(1)}, f32[2,3,4,40,256]{4,3,2,1,0:T(8,128)S(1)}, f32[2,3,4,40,256]{4,3,2,1,0:T(8,128)S(1)}, f32[2,3,4,40,...) custom-call(f32[8]{0:T(128)S(1)} %stack.35.refs_0_, ...), custom_call_target="tpu_custom_call", output_to_operand_aliasing={{0}: (6, {}), {1}: (7, {}), {2}: (8, {}), {3}: (9, {}), {4}... | custom-call | tf_op jit(solution)/shard_map/pallas_call | solution.py:340
  78.7 1.3 %collective-permute-start.9 = (f32[48,8,256]{2,1,0:T(8,128)S(1)}, f32[48,8,256]{2,1,0:T(8,128)S(1)}, u32[]{:S(2)}, u32[]{:S(2)}) collective-permute-start(f32[48,8,256]{2,1,0:T(8,128)S(1)} %get-tuple-element.155), channel_id=1, source_target_pairs={{0,1},{1,0},{2,3},{3,2},{4,5},{5,4},{6,7},{7,6},{8,9},{9,8},{10,11... | collective-permute-start | bytes 1179656 | tf_op jit(solution)/shard_map/ppermute | solution.py:354
  80.0 1.3 %collective-permute-done.9.refs_2_ = f32[48,8,256]{2,1,0:T(8,128)S(1)} collective-permute-done((f32[48,8,256]{2,1,0:T(8,128)S(1)}, f32[48,8,256]{2,1,0:T(8,128)S(1)}, u32[]{:S(2)}, u32[]{:S(2)}) %collective-permute-start.9) | collective-permute-done | bytes 393248 | tf_op jit(solution)/shard_map/ppermute | solution.py:354
  81.3 1.9 %shard_map.166 = (f32[2,3,4,40,256]{4,3,2,1,0:T(8,128)S(1)}, f32[2,3,4,40,256]{4,3,2,1,0:T(8,128)S(1)}, f32[2,3,4,40,256]{4,3,2,1,0:T(8,128)S(1)}, f32[2,3,4,40,...) custom-call(f32[8]{0:T(128)S(1)} %stack.35.refs_0_, ...), custom_call_target="tpu_custom_call", output_to_operand_aliasing={{0}: (3, {}), {1}: (4, {}), {2}: (5, {}), {3}: (6, {}), {4}... | custom-call | tf_op jit(solution)/shard_map/pallas_call | solution.py:340
  85.8 1.5 %collective-permute-start.10 = (f32[272,256]{1,0:T(8,128)}, f32[272,256]{1,0:T(8,128)S(1)}, u32[]{:S(2)}, u32[]{:S(2)}) collective-permute-start(f32[272,256]{1,0:T(8,128)} %get-tuple-element.161), channel_id=1, source_target_pairs={{0,2},{2,0},{4,6},{6,4},{8,10},{10,8},{12,14},{14,12},{1,3},{3,1},... | collective-permute-start | bytes 835592 | tf_op jit(solution)/shard_map/ppermute | solution.py:354
  87.2 3.3 %collective-permute-start.11 = (f32[272,256]{1,0:T(8,128)}, f32[272,256]{1,0:T(8,128)}, u32[]{:S(2)}, u32[]{:S(2)}) collective-permute-start(f32[272,256]{1,0:T(8,128)} %get-tuple-element.162), channel_id=1, source_target_pairs={{2,4},{4,2},{6,8},{8,6},{10,12},{12,10},{14,0},{0,14},{3,5},{5,3},... | collective-permute-start | bytes 835592 | tf_op jit(solution)/shard_map/ppermute | solution.py:354
  93.3 6.5 %collective-permute-done.10.refs_2_ = f32[272,256]{1,0:T(8,128)S(1)} collective-permute-done((f32[272,256]{1,0:T(8,128)}, f32[272,256]{1,0:T(8,128)S(1)}, u32[]{:S(2)}, u32[]{:S(2)}) %collective-permute-start.10) | collective-permute-done | bytes 278560 | tf_op jit(solution)/shard_map/ppermute | solution.py:354
  99.8 3.7 %shard_map.168 = (f32[2,3,4,40,256]{4,3,2,1,0:T(8,128)S(1)}, f32[2,3,4,40,256]{4,3,2,1,0:T(8,128)S(1)}, f32[2,3,4,40,256]{4,3,2,1,0:T(8,128)S(1)}, f32[2,3,4,40,...) custom-call(f32[8]{0:T(128)S(1)} %stack.35.refs_0_, ...), custom_call_target="tpu_custom_call", output_to_operand_aliasing={{0}: (6, {}), {1}: (7, {}), {2}: (8, {}), {3}: (9, {}), {4}... | custom-call | tf_op jit(solution)/shard_map/pallas_call | solution.py:340
  103.5 1.2 %collective-permute-start.12 = (f32[2,4,8,128]{3,2,1,0:T(8,128)S(1)}, f32[2,4,8,128]{3,2,1,0:T(8,128)S(1)}, u32[]{:S(2)}, u32[]{:S(2)}) collective-permute-start(f32[2,4,8,128]{3,2,1,0:T(8,128)S(1)} %get-tuple-element.180), channel_id=1, source_target_pairs={{0,1},{1,0},{2,3},{3,2},{4,5},{5,4},{6,7},{7,6},{8,9},{9,8},{10,11... | collective-permute-start | bytes 98312 | tf_op jit(solution)/shard_map/ppermute | solution.py:354
  (73 shorter events, 26.9 us)
Async XLA Ops:
  0.6 1.1 %copy-start.10 = (f32[2,3,4,32,256]{4,3,2,1,0:T(8,128)S(1)}, f32[2,3,4,32,256]{4,3,2,1,0:T(8,128)}, u32[]{:S(2)}) copy-start(f32[2,3,4,32,256]{4,3,2,1,0:T(8,128)} %e_in.1) | copy-start | bytes 2359300
  1.8 1.1 %copy-start.11 = (f32[2,3,4,32,256]{4,3,2,1,0:T(8,128)S(1)}, f32[2,3,4,32,256]{4,3,2,1,0:T(8,128)}, u32[]{:S(2)}) copy-start(f32[2,3,4,32,256]{4,3,2,1,0:T(8,128)} %h_in.1) | copy-start | bytes 2359300
  2.9 1.1 %copy-start.12 = (f32[2,3,4,32,256]{4,3,2,1,0:T(8,128)S(1)}, f32[2,3,4,32,256]{4,3,2,1,0:T(8,128)}, u32[]{:S(2)}) copy-start(f32[2,3,4,32,256]{4,3,2,1,0:T(8,128)} %p_in.1) | copy-start | bytes 2359300
  4.0 1.1 %copy-start.13 = (f32[2,3,4,32,256]{4,3,2,1,0:T(8,128)S(1)}, f32[2,3,4,32,256]{4,3,2,1,0:T(8,128)}, u32[]{:S(2)}) copy-start(f32[2,3,4,32,256]{4,3,2,1,0:T(8,128)} %j_in.1) | copy-start | bytes 2359300
  6.1 8.7 %copy-start.15 = (s32[4,32,256]{2,1,0:T(8,128)S(1)}, s32[4,32,256]{2,1,0:T(8,128)}, u32[]{:S(2)}) copy-start(s32[4,32,256]{2,1,0:T(8,128)} %mat.3) | copy-start | bytes 393220
  8.1 9.0 %collective-permute-start = (f32[52,8,256]{2,1,0:T(8,128)}, f32[52,8,256]{2,1,0:T(8,128)S(1)}, u32[]{:S(2)}, u32[]{:S(2)}) collective-permute-start(f32[52,8,256]{2,1,0:T(8,128)} %get-tuple-element.93), channel_id=1, source_target_pairs={{0,1},{1,0},{2,3},{3,2},{4,5},{5,4},{6,7},{7,6},{8,9},{9,8},{10,11... | collective-permute-start | bytes 1277960 | tf_op jit(solution)/shard_map/ppermute | solution.py:354
  9.5 5.3 %copy-start.22 = (f32[4]{0:T(128)S(1)}, f32[4]{0:T(128)}, u32[]{:S(2)}) copy-start(f32[4]{0:T(128)} %refs_7_.1) | copy-start | bytes 52
  17.1 1.2 %copy-start.1 = (f32[2,3,4,40,256]{4,3,2,1,0:T(8,128)S(1)}, f32[2,3,4,40,256]{4,3,2,1,0:T(8,128)}, u32[]{:S(2)}) copy-start(f32[2,3,4,40,256]{4,3,2,1,0:T(8,128)} %copy-done) | copy-start | bytes 2949124
  21.6 17.4 %collective-permute-start.1 = (f32[312,256]{1,0:T(8,128)S(1)}, f32[312,256]{1,0:T(8,128)S(1)}, u32[]{:S(2)}, u32[]{:S(2)}) collective-permute-start(f32[312,256]{1,0:T(8,128)S(1)} %get-tuple-element.98), channel_id=1, source_target_pairs={{0,2},{2,0},{4,6},{6,4},{8,10},{10,8},{12,14},{14,12},{1,3},{3,1},... | collective-permute-start | bytes 958472 | tf_op jit(solution)/shard_map/ppermute | solution.py:354
  24.3 14.8 %collective-permute-start.2 = (f32[312,256]{1,0:T(8,128)S(1)}, f32[312,256]{1,0:T(8,128)S(1)}, u32[]{:S(2)}, u32[]{:S(2)}) collective-permute-start(f32[312,256]{1,0:T(8,128)S(1)} %get-tuple-element.99), channel_id=1, source_target_pairs={{2,4},{4,2},{6,8},{8,6},{10,12},{12,10},{14,0},{0,14},{3,5},{5,3},... | collective-permute-start | bytes 958472 | tf_op jit(solution)/shard_map/ppermute | solution.py:354
  27.6 1.1 %copy-start.7 = (f32[4,4,40,256]{3,2,1,0:T(8,128)S(1)}, f32[4,4,40,256]{3,2,1,0:T(8,128)}, u32[]{:S(2)}) copy-start(f32[4,4,40,256]{3,2,1,0:T(8,128)} %copy-done.6) | copy-start | bytes 1966084
  40.7 2.0 %collective-permute-start.3 = (f32[48,8,256]{2,1,0:T(8,128)S(1)}, f32[48,8,256]{2,1,0:T(8,128)S(1)}, u32[]{:S(2)}, u32[]{:S(2)}) collective-permute-start(f32[48,8,256]{2,1,0:T(8,128)S(1)} %get-tuple-element.112), channel_id=1, source_target_pairs={{0,1},{1,0},{2,3},{3,2},{4,5},{5,4},{6,7},{7,6},{8,9},{9,8},{10,11... | collective-permute-start | bytes 1179656 | tf_op jit(solution)/shard_map/ppermute | solution.py:354
  43.9 13.9 %collective-permute-start.4 = (f32[272,256]{1,0:T(8,128)S(1)}, f32[272,256]{1,0:T(8,128)S(1)}, u32[]{:S(2)}, u32[]{:S(2)}) collective-permute-start(f32[272,256]{1,0:T(8,128)S(1)} %get-tuple-element.118), channel_id=1, source_target_pairs={{0,2},{2,0},{4,6},{6,4},{8,10},{10,8},{12,14},{14,12},{1,3},{3,1},... | collective-permute-start | bytes 835592 | tf_op jit(solution)/shard_map/ppermute | solution.py:354
  45.4 12.4 %collective-permute-start.5 = (f32[272,256]{1,0:T(8,128)S(1)}, f32[272,256]{1,0:T(8,128)S(1)}, u32[]{:S(2)}, u32[]{:S(2)}) collective-permute-start(f32[272,256]{1,0:T(8,128)S(1)} %get-tuple-element.119), channel_id=1, source_target_pairs={{2,4},{4,2},{6,8},{8,6},{10,12},{12,10},{14,0},{0,14},{3,5},{5,3},... | collective-permute-start | bytes 835592 | tf_op jit(solution)/shard_map/ppermute | solution.py:354
  59.4 2.6 %collective-permute-start.6 = (f32[48,8,256]{2,1,0:T(8,128)S(1)}, f32[48,8,256]{2,1,0:T(8,128)S(1)}, u32[]{:S(2)}, u32[]{:S(2)}) collective-permute-start(f32[48,8,256]{2,1,0:T(8,128)S(1)} %get-tuple-element.134), channel_id=1, source_target_pairs={{0,1},{1,0},{2,3},{3,2},{4,5},{5,4},{6,7},{7,6},{8,9},{9,8},{10,11... | collective-permute-start | bytes 1179656 | tf_op jit(solution)/shard_map/ppermute | solution.py:354
  63.2 13.9 %collective-permute-start.7 = (f32[272,256]{1,0:T(8,128)S(1)}, f32[272,256]{1,0:T(8,128)S(1)}, u32[]{:S(2)}, u32[]{:S(2)}) collective-permute-start(f32[272,256]{1,0:T(8,128)S(1)} %get-tuple-element.140), channel_id=1, source_target_pairs={{0,2},{2,0},{4,6},{6,4},{8,10},{10,8},{12,14},{14,12},{1,3},{3,1},... | collective-permute-start | bytes 835592 | tf_op jit(solution)/shard_map/ppermute | solution.py:354
  64.7 12.4 %collective-permute-start.8 = (f32[272,256]{1,0:T(8,128)S(1)}, f32[272,256]{1,0:T(8,128)S(1)}, u32[]{:S(2)}, u32[]{:S(2)}) collective-permute-start(f32[272,256]{1,0:T(8,128)S(1)} %get-tuple-element.141), channel_id=1, source_target_pairs={{2,4},{4,2},{6,8},{8,6},{10,12},{12,10},{14,0},{0,14},{3,5},{5,3},... | collective-permute-start | bytes 835592 | tf_op jit(solution)/shard_map/ppermute | solution.py:354
  78.7 2.6 %collective-permute-start.9 = (f32[48,8,256]{2,1,0:T(8,128)S(1)}, f32[48,8,256]{2,1,0:T(8,128)S(1)}, u32[]{:S(2)}, u32[]{:S(2)}) collective-permute-start(f32[48,8,256]{2,1,0:T(8,128)S(1)} %get-tuple-element.155), channel_id=1, source_target_pairs={{0,1},{1,0},{2,3},{3,2},{4,5},{5,4},{6,7},{7,6},{8,9},{9,8},{10,11... | collective-permute-start | bytes 1179656 | tf_op jit(solution)/shard_map/ppermute | solution.py:354
  81.3 9.1 %copy-start.23 = (f32[2,16,32]{2,1,0:T(8,128)S(1)}, f32[2,16,32]{2,1,0:T(8,128)}, u32[]{:S(2)}) copy-start(f32[2,16,32]{2,1,0:T(8,128)} %constant.38.clone) | copy-start | bytes 12292
  85.8 14.1 %collective-permute-start.10 = (f32[272,256]{1,0:T(8,128)}, f32[272,256]{1,0:T(8,128)S(1)}, u32[]{:S(2)}, u32[]{:S(2)}) collective-permute-start(f32[272,256]{1,0:T(8,128)} %get-tuple-element.161), channel_id=1, source_target_pairs={{0,2},{2,0},{4,6},{6,4},{8,10},{10,8},{12,14},{14,12},{1,3},{3,1},... | collective-permute-start | bytes 835592 | tf_op jit(solution)/shard_map/ppermute | solution.py:354
  87.2 12.6 %collective-permute-start.11 = (f32[272,256]{1,0:T(8,128)}, f32[272,256]{1,0:T(8,128)}, u32[]{:S(2)}, u32[]{:S(2)}) collective-permute-start(f32[272,256]{1,0:T(8,128)} %get-tuple-element.162), channel_id=1, source_target_pairs={{2,4},{4,2},{6,8},{8,6},{10,12},{12,10},{14,0},{0,14},{3,5},{5,3},... | collective-permute-start | bytes 835592 | tf_op jit(solution)/shard_map/ppermute | solution.py:354
  90.5 1.2 %copy-start.3 = (f32[2,3,4,40,256]{4,3,2,1,0:T(8,128)S(1)}, f32[2,3,4,40,256]{4,3,2,1,0:T(8,128)}, u32[]{:S(2)}) copy-start(f32[2,3,4,40,256]{4,3,2,1,0:T(8,128)} %copy-done.2) | copy-start | bytes 2949124
  92.8 7.0 %copy-start.17 = (f32[2,2,40,256]{3,2,1,0:T(8,128)S(1)}, f32[2,2,40,256]{3,2,1,0:T(8,128)}, u32[]{:S(2)}) copy-start(f32[2,2,40,256]{3,2,1,0:T(8,128)} %copy-done.16) | copy-start | bytes 491524
  103.5 2.1 %collective-permute-start.12 = (f32[2,4,8,128]{3,2,1,0:T(8,128)S(1)}, f32[2,4,8,128]{3,2,1,0:T(8,128)S(1)}, u32[]{:S(2)}, u32[]{:S(2)}) collective-permute-start(f32[2,4,8,128]{3,2,1,0:T(8,128)S(1)} %get-tuple-element.180), channel_id=1, source_target_pairs={{0,1},{1,0},{2,3},{3,2},{4,5},{5,4},{6,7},{7,6},{8,9},{9,8},{10,11... | collective-permute-start | bytes 98312 | tf_op jit(solution)/shard_map/ppermute | solution.py:354
  (14 other events, 11.5 us)
where the time goes:
time: 107 us; the launch traced here: 106 us
  waiting for transfers between devices  38.4 us (36%)
  starting transfers between devices  24.7 us (23%)
  local copies, waits for them, and re-layouts  19 us (18%)
  Pallas kernels  18.2 us (17%)
  between operations  6.02 us (6%)
    ppermute x13, waiting for transfers between devices, swap(): lax.ppermute(block, axis, [q for a, b in pairs for q in ((a, b), (b, a))])  38.4 us
    ppermute x13, starting transfers between devices, swap(): lax.ppermute(block, axis, [q for a, b in pairs for q in ((a, b), (b, a))])  24.7 us
    pallas_call x14, Pallas kernels, call(): pl.pallas_call(body, out_shape=shapes, in_specs=[sm if i in smem else vm...  18.2 us
    unnamed x51, local copies, waits for them, and re-layouts  18.2 us
  transfers between devices with their start and end apart: 13, of which 8 were waited for; matrix products, arithmetic and copies ran while one was open for 1% of the time, Pallas kernels for 3%

commit v1 on v0

--- a/solution.py
+++ b/solution.py
@@ -13,7 +13,7 @@
 HARM = 8
 EDGE = 8
 courant = 0.5
-VMEM_LIMIT = 24 << 20
+VMEM_LIMIT = 8 << 20
 
 
 def next_y(v):
@@ -65,13 +65,21 @@
                     out[((r * 2 + g) * comps + k) * planes + x] = tile
 
 
-def unpack_edges(recv, fields, phase, rows):
+def wrap_phase(cs, axis, name, up):
+    at, count = lax.axis_index(name), lax.axis_size(name)
+    wraps = at == (count - 1 if up else 0)
+    sine = cs[2 + axis, 0:1]
+    return jnp.where(wraps, cs[axis, 0:1], 1.0), jnp.where(wraps, sine if up else 0.0 - sine, 0.0)
+
+
+def unpack_edges(recv, fields, cs, rows):
     e, h, p, j = fields
+    up, dn = wrap_phase(cs, 1, "gy", True), wrap_phase(cs, 1, "gy", False)
     comps, planes = e.shape[1:3]
     depth = e.shape[4]
     row = lax.broadcasted_iota(jnp.int32, (8, depth), 0)
-    cos_v = jnp.where(row < 4, phase[4], phase[6])
-    sin_v = jnp.where(row < 4, phase[5], phase[7])
+    cos_v = jnp.where(row < 4, up[0], dn[0])
+    sin_v = jnp.where(row < 4, up[1], dn[1])
     for g, (one, two) in enumerate(((e, h), (p, j))):
         for k in range(comps):
             for x in range(planes):
@@ -131,14 +139,36 @@
     rec[r, x] = jnp.where(lane == step, pltpu.roll(top, (step + 1) % 128, 1), rec[r, x])
 
 
-def start_body(rows, e_in, h_in, p_in, j_in, mat, e, h, p, j, edges):
-    for src, dst in ((e_in, e), (h_in, h), (p_in, p), (j_in, j)):
-        dst[:, :, :, 0:rows] = src[...]
+def start_body(rows, e_in, h_in, p_in, j_in, mat_in, e, h, p, j, mat, edges, sems):
+    pairs = [(src, dst.at[:, :, :, 0:rows]) for src, dst in ((e_in, e), (h_in, h), (p_in, p), (j_in, j))]
+    copies = [pltpu.make_async_copy(src, dst, sems.at[i]) for i, (src, dst) in enumerate(pairs + [(mat_in, mat)])]
+    for c in copies:
+        c.start()
+    for dst in (e, h, p, j):
         dst[:, :, :, rows:] = jnp.zeros(dst.shape[:3] + (EDGE, dst.shape[4]), jnp.float32)
-    pack_edges((e_in, h_in, p_in, j_in), edges, rows)
-    base = 2 * 2 * 3 * e_in.shape[2]
-    for x in range(e_in.shape[2]):
+    for c in copies:
+        c.wait()
+    pack_edges((e, h, p, j), edges, rows)
+    base = 2 * 2 * 3 * e.shape[2]
+    for x in range(e.shape[2]):
         edges[base + x] = edge_rows(mat, (x,), rows).astype(jnp.float32)
+
+
+def store_body(rows, e, h, p, j, e_out, h_out, p_out, j_out, sems):
+    pairs = ((e, e_out), (h, h_out), (p, p_out), (j, j_out))
+    copies = [
+        pltpu.make_async_copy(src.at[:, :, :, 0:rows], dst, sems.at[i]) for i, (src, dst) in enumerate(pairs)
+    ]
+    for c in copies:
+        c.start()
+    for c in copies:
+        c.wait()
+
+
+def panel_body(own, other, out):
+    for r in range(2):
+        for x in range(own.shape[1]):
+            out[r, :, x] = jnp.transpose(own[r, x] + other[r, x])[0:STEPS]
 
 
 def cell_tables(kind, pole_of, eps, dec, frq, stg):
@@ -152,7 +182,12 @@
     return vals
 
 
-def coef_body(rows, mat, pole_of, eps, dec, frq, stg, coef):
+def coef_body(rows, mat, pole_of, eps, dec, frq, stg, bloch, coef, cs, rec):
+    rec[...] = jnp.zeros(rec.shape, jnp.float32)
+    for i in range(2):
+        turns = jnp.full(cs.shape[1:], bloch[i], jnp.float32)
+        cs[i] = jnp.cos(turns)
+        cs[2 + i] = jnp.sin(turns)
     for x in range(mat.shape[0]):
         for y in range(0, rows, 8):
             vals = cell_tables(mat[x, y : y + 8], pole_of, eps, dec, frq, stg)
@@ -164,15 +199,15 @@
 
 def send_body(rows, first, refs):
     refs = list(refs)
-    phase, par, edges = refs[0:3]
-    refs = refs[3:]
+    cs, edges = refs[0:2]
+    refs = refs[2:]
     if first:
         pole_of, eps, dec, frq, stg = refs[0:5]
         refs = refs[5:]
     e, h, p, j, coef, e0, ev, od, msg = refs[5:]
     planes = e.shape[2]
     last = planes - 1
-    unpack_edges(edges, (e, h, p, j), phase, rows)
+    unpack_edges(edges, (e, h, p, j), cs, rows)
     if first:
         base = 2 * 2 * 3 * planes
         for x in range(planes):
@@ -180,7 +215,8 @@
             vals = cell_tables(kind, pole_of, eps, dec, frq, stg)
             for i in range(4):
                 coef[i, x, rows:] = vals[i]
-    up, dn = par[0], 1 - par[0]
+    up = lax.axis_index("gx") % 2
+    dn = 1 - up
     half = 4 * rows
     for r in range(2):
         tiles_d, tiles_u = [], []
@@ -240,8 +276,8 @@
 
 def finish_body(rows, step, first, final, refs):
     refs = list(refs)
-    phase, par, ev, od, e0 = refs[0:5]
-    refs = refs[5:]
+    cs, ev, od, e0 = refs[0:4]
+    refs = refs[4:]
     if not first:
         far_in = refs[0]
         refs = refs[1:]
@@ -255,8 +291,8 @@
     else:
         far = far_in
     if final:
-        e_out, h_out, p_out, j_out, wave, harm = refs[0:6]
-        refs = refs[6:]
+        waves, harm = refs[0:2]
+        refs = refs[2:]
     else:
         edges = refs[0]
         refs = refs[1:]
@@ -266,7 +302,8 @@
     half = 4 * rows
     msg[0] = ev[...]
     msg[1] = od[...]
-    fa, fb = par[0], 1 - par[0]
+    fa = lax.axis_index("gx") % 2
+    fb = 1 - fa
     if first:
         far[0] = msg[fb, 2 * half + 16 : 2 * half + 16 + rows + EDGE]
         far[1] = msg[fa, 2 * half + 16 : 2 * half + 16 + rows + EDGE]
@@ -287,7 +324,7 @@
             res.append((turn((raw[0][0], raw[1][0]), cos_v, sin_v), turn((raw[0][1], raw[1][1]), cos_v, sin_v)))
         return res
 
-    above = arrived(fa, phase[0], phase[1])
+    above = arrived(fa, *wrap_phase(cs, 0, "gx", True))
     for r in range(2):
         a0y, a0z = above[0][0][r], above[1][0][r]
         dhy, dhz = courant * a0z, 0.0 - courant * a0y
@@ -303,7 +340,7 @@
         magnetic_full(e, h, r, last - 1, (e[r, 1, last], e[r, 2, last]))
         magnetic_full(e, h, r, last, (a1y, a1z))
         polarize_step(e, p, j, coef, r, last)
-    below = arrived(fb, phase[2], phase[3])
+    below = arrived(fb, *wrap_phase(cs, 0, "gx", False))
     for r in range(2):
         dhy, dhz = courant * e0[r, 1], 0.0 - courant * e0[r, 0]
         e[r, 1, 0] = e[r, 1, 0] + coef[0, 0] * (below[1][0][r] + dhz)
@@ -322,28 +359,29 @@
     if not final:
         pack_edges((e, h, p, j), edges, rows)
         return
-    for src, dst in ((e, e_out), (h, h_out), (p, p_out), (j, j_out)):
-        dst[...] = src[:, :, :, 0:rows]
+    wave = waves[lax.axis_index("gy")]
     for x in range(planes):
         re, im = (
-            jnp.dot(wave[...], rec[r, x], precision=lax.Precision.HIGHEST, preferred_element_type=jnp.float32)
+            jnp.dot(wave, rec[r, x], precision=lax.Precision.HIGHEST, preferred_element_type=jnp.float32)
             for r in range(2)
         )
         harm[0, x] = re[0:HARM] + im[HARM:]
         harm[1, x] = im[0:HARM] - re[HARM:]
 
 
-def call(body, ins, outs, aliases=None, smem=(), scratch=()):
+def call(body, ins, outs, aliases=None, smem=(), hbm_in=(), hbm_out=False, scratch=(), cost=0):
     shapes = [jax.ShapeDtypeStruct(s, d) for s, d in outs]
     vm = pl.BlockSpec(memory_space=pltpu.VMEM)
     sm = pl.BlockSpec(memory_space=pltpu.SMEM)
+    hbm = pl.BlockSpec(memory_space=pltpu.HBM)
     return pl.pallas_call(
         body,
         out_shape=shapes,
-        in_specs=[sm if i in smem else vm for i in range(len(ins))],
-        out_specs=[vm] * len(outs),
+        in_specs=[sm if i in smem else hbm if i in hbm_in else vm for i in range(len(ins))],
+        out_specs=[hbm if hbm_out else vm] * len(outs),
         input_output_aliases=aliases or {},
         scratch_shapes=list(scratch),
+        cost_estimate=pl.CostEstimate(flops=cost, bytes_accessed=cost, transcendentals=0),
         compiler_params=pltpu.CompilerParams(vmem_limit_bytes=VMEM_LIMIT),
     )(*ins)
 
@@ -360,54 +398,45 @@
     parts, comps, planes, rows, depth = electric.shape
     count_x, count_y = lax.axis_size("gx"), lax.axis_size("gy")
     assert count_x % 2 == 0 and count_y == 2 and planes >= 4
-    where_x, where_y = lax.axis_index("gx"), lax.axis_index("gy")
     width_y = rows * count_y
     f32 = jnp.float32
     ext = (rows + EDGE, depth)
-    cos_b, sin_b = jnp.cos(bloch), jnp.sin(bloch)
-
-    def hop(at, edge, axis, sign):
-        return [jnp.where(at == edge, cos_b[axis], 1.0), jnp.where(at == edge, sign * sin_b[axis], 0.0)]
-
-    phase = jnp.stack(
-        hop(where_x, count_x - 1, 0, 1.0)
-        + hop(where_x, 0, 0, -1.0)
-        + hop(where_y, count_y - 1, 1, 1.0)
-        + hop(where_y, 0, 1, -1.0)
-    )
-    par = jnp.reshape(where_x % 2, (1,)).astype(jnp.int32)
     angle = 2.0 * math.pi / width_y * (np.arange(HARM)[:, None] * np.arange(width_y)[None, :] % width_y)
     waves = np.concatenate([np.cos(angle), np.sin(angle)]) / math.sqrt(width_y)
-    waves = np.stack(np.split(waves, count_y, axis=1)).astype(np.float32)
-    wave = lax.dynamic_index_in_dim(jnp.asarray(waves), where_y, 0, keepdims=False)
+    waves = jnp.asarray(np.stack(np.split(waves, count_y, axis=1)).astype(np.float32))
 
     state_shape = ((parts, comps, planes) + ext, f32)
     coef_shape = ((4, planes) + ext, f32)
     tiles = 2 * 2 * comps * planes
-    e, h, p, j, edges = call(
+    e, h, p, j, mat, edges = call(
         functools.partial(start_body, rows),
         (electric, magnetic, polarize, currents, material),
-        [state_shape] * 4 + [((tiles + planes, 8, depth), f32)],
+        [state_shape] * 4 + [(material.shape, material.dtype), ((tiles + planes, 8, depth), f32)],
+        hbm_in=range(5),
+        scratch=[pltpu.SemaphoreType.DMA((5,))],
     )
     tables = (pole_of, eps_inf, pole_decay, pole_freq, pole_strength)
-    (coef,) = call(
-        functools.partial(coef_body, rows), (material,) + tables, [coef_shape], smem=range(1, 6)
+    coef, cs, rec = call(
+        functools.partial(coef_body, rows),
+        (mat,) + tables + (bloch,),
+        [coef_shape, ((4, 8, depth), f32), ((2, planes, rows, 128), f32)],
+        smem=range(1, 7),
+        cost=1 << 20,
     )
-    rec = jnp.zeros((2, planes, rows, 128), f32)
     far = None
     for step in range(0, STEPS, 2):
         first, final = step == 0, step == STEPS - 2
         edges = swap(edges, "gy", 0)
         size = 8 * rows + 16 + (rows + EDGE if first else 0)
         extra = tables if first else ()
-        ins = (phase, par, edges) + extra + (e, h, p, j, coef)
-        n = 3 + len(extra)
+        ins = (cs, edges) + extra + (e, h, p, j, coef)
+        n = 2 + len(extra)
         e, h, p, j, coef, e0, ev, od = call(
             lambda *refs, first=first: send_body(rows, first, refs),
             ins,
             [state_shape] * 4 + [coef_shape, ((2, 2) + ext, f32)] + [((size, depth), f32)] * 2,
             {n + i: i for i in range(5)},
-            smem=(0, 1) + tuple(range(3, n)),
+            smem=tuple(range(2, n)),
             scratch=[pltpu.VMEM((2, size, depth), f32)],
         )
         ev, od = swap(ev, "gx", 0), swap(od, "gx", 1)
@@ -416,16 +445,17 @@
             (e, h, p, j, coef, rec),
             [state_shape] * 4 + [coef_shape, (rec.shape, f32)],
             {i: i for i in range(6)},
+            cost=1 << 20,
         )
-        ins = (phase, par, ev, od, e0) + (() if first else (far,))
+        ins = (cs, ev, od, e0) + (() if first else (far,))
         n = len(ins)
         ins = ins + (e, h, p, j, rec, coef)
         outs = [state_shape] * 4 + [(rec.shape, f32), coef_shape]
         if first:
             outs.append(((2,) + ext, f32))
         if final:
-            ins = ins + (wave,)
-            outs += [(electric.shape, f32)] * 4 + [((2, planes, HARM, 128), f32)]
+            ins = ins + (waves,)
+            outs.append(((2, planes, HARM, 128), f32))
         else:
             outs.append(((tiles, 8, depth), f32))
 
@@ -437,7 +467,7 @@
             finish_body(rows, step, first, final, refs)
 
         res = call(
-            body, ins, outs, {n + i: i for i in range(6)}, smem=(0, 1), scratch=[pltpu.VMEM((2, size, depth), f32)]
+            body, ins, outs, {n + i: i for i in range(6)}, scratch=[pltpu.VMEM((2, size, depth), f32)]
         )
         e, h, p, j, rec, coef = res[0:6]
         res = res[6:]
@@ -446,10 +476,18 @@
             res = res[1:]
         if not final:
             edges = res[0]
-    *fields, harm = res
-    harm = harm + swap(harm, "gy", 0)
-    history = jnp.transpose(harm[..., :STEPS], (0, 3, 2, 1))
-    return (*fields, history)
+    (harm,) = res
+    other = swap(harm, "gy", 0)
+    fields = call(
+        functools.partial(store_body, rows),
+        (e, h, p, j),
+        [(electric.shape, f32)] * 4,
+        hbm_out=True,
+        scratch=[pltpu.SemaphoreType.DMA((4,))],
+        cost=1 << 22,
+    )
+    (panel,) = call(panel_body, (harm, other), [((2, STEPS, planes, HARM), f32)])
+    return (*fields, jnp.transpose(panel, (0, 1, 3, 2)))
 
 
 def solution(mesh):

time: 107 us -> 87.3 us (0.82)
  local copies, waits for them, and re-layouts: 19 us -> 6 us
  between operations: 6.02 us -> 0.81 us
  Pallas kernels: 18.2 us -> 14.7 us
  waiting for transfers between devices: 38.4 us -> 40.6 us
    unnamed x51 -> x24, local copies, waits for them, and re-layouts: 18.2 us -> 6 us
    pallas_call x14 -> x16, Pallas kernels: 18.2 us -> 14.7 us  [call(): pl.pallas_call(body, out_shape=shapes, in_specs=[sm if i in smem else hbm...]
    ppermute x13, waiting for transfers between devices: 38.4 us -> 40.6 us  [swap(): lax.ppermute(block, axis, [q for a, b in pairs for q in ((a, b), (b, a))])]
  transfers between devices with their start and end apart: 13 -> 13, of which waited for: 8 -> 8; matrix products, arithmetic and copies ran while one was open for 1% -> 0% of each run, Pallas kernels for 3% -> 6%
where the time goes in v1:
time: 87.3 us; the launch traced here: 87 us
  waiting for transfers between devices  40.6 us (47%)
  starting transfers between devices  24.9 us (29%)
  Pallas kernels  14.7 us (17%)
  local copies, waits for them, and re-layouts  6 us (7%)
    ppermute x13, waiting for transfers between devices, swap(): lax.ppermute(block, axis, [q for a, b in pairs for q in ((a, b), (b, a))])  40.6 us
    ppermute x13, starting transfers between devices, swap(): lax.ppermute(block, axis, [q for a, b in pairs for q in ((a, b), (b, a))])  24.9 us
    pallas_call x16, Pallas kernels, call(): pl.pallas_call(body, out_shape=shapes, in_specs=[sm if i in smem else hbm...  14.7 us
    unnamed x24, local copies, waits for them, and re-layouts  6 us
  transfers between devices with their start and end apart: 13, of which 8 were waited for; matrix products, arithmetic and copies ran while one was open for 0% of the time, Pallas kernels for 6%

profile of v1, /device:TPU:1, one launch (start us, length us, event | category | flops | bytes accessed | tf_op | source)
XLA Modules:
  0.0 87.0 jit_solution(8690329292742285690)
XLA Ops:
  8.6 1.4 %shard_map.157 = (f32[2,3,4,40,256]{4,3,2,1,0:T(8,128)S(1)}, f32[2,3,4,40,256]{4,3,2,1,0:T(8,128)S(1)}, f32[2,3,4,40,256]{4,3,2,1,0:T(8,128)S(1)}, f32[2,3,4,40,...) custom-call(f32[4,8,256]{2,1,0:T(8,128)S(1)} %get-tuple-element.102., ...), custom_call_target="tpu_custom_call", output_to_operand_aliasing={{0}: (7, {}), {1}: (8, {}), {2}: (9, {}), {3}: (10, {}), {4... | custom-call | tf_op jit(solution)/shard_map/pallas_call | solution.py:377
  10.0 2.4 %collective-permute-start.1 = (f32[312,256]{1,0:T(8,128)S(1)}, f32[312,256]{1,0:T(8,128)S(1)}, u32[]{:S(2)}, u32[]{:S(2)}) collective-permute-start(f32[312,256]{1,0:T(8,128)S(1)} %get-tuple-element.109), channel_id=1, source_target_pairs={{0,2},{2,0},{4,6},{6,4},{8,10},{10,8},{12,14},{14,12},{1,3},{3,1},... | collective-permute-start | bytes 958472 | tf_op jit(solution)/shard_map/ppermute | solution.py:392
  12.4 3.3 %collective-permute-start.2 = (f32[312,256]{1,0:T(8,128)S(1)}, f32[312,256]{1,0:T(8,128)S(1)}, u32[]{:S(2)}, u32[]{:S(2)}) collective-permute-start(f32[312,256]{1,0:T(8,128)S(1)} %get-tuple-element.110), channel_id=1, source_target_pairs={{2,4},{4,2},{6,8},{8,6},{10,12},{12,10},{14,0},{0,14},{3,5},{5,3},... | collective-permute-start | bytes 958472 | tf_op jit(solution)/shard_map/ppermute | solution.py:392
  16.3 10.6 %collective-permute-done.1.refs_1_ = f32[312,256]{1,0:T(8,128)S(1)} collective-permute-done((f32[312,256]{1,0:T(8,128)S(1)}, f32[312,256]{1,0:T(8,128)S(1)}, u32[]{:S(2)}, u32[]{:S(2)}) %collective-permute-start.1) | collective-permute-done | bytes 319520 | tf_op jit(solution)/shard_map/ppermute | solution.py:392
  26.9 1.2 %shard_map.159 = (f32[2,3,4,40,256]{4,3,2,1,0:T(8,128)S(1)}, f32[2,3,4,40,256]{4,3,2,1,0:T(8,128)S(1)}, f32[2,3,4,40,256]{4,3,2,1,0:T(8,128)S(1)}, f32[2,3,4,40,...) custom-call(f32[4,8,256]{2,1,0:T(8,128)S(1)} %get-tuple-element.102., ...), custom_call_target="tpu_custom_call", output_to_operand_aliasing={{0}: (4, {}), {1}: (5, {}), {2}: (6, {}), {3}: (7, {}), {4}... | custom-call | tf_op jit(solution)/shard_map/pallas_call | solution.py:377
  29.1 1.3 %collective-permute-done.3.refs_1_ = f32[48,8,256]{2,1,0:T(8,128)S(1)} collective-permute-done((f32[48,8,256]{2,1,0:T(8,128)S(1)}, f32[48,8,256]{2,1,0:T(8,128)S(1)}, u32[]{:S(2)}, u32[]{:S(2)}) %collective-permute-start.3) | collective-permute-done | bytes 393248 | tf_op jit(solution)/shard_map/ppermute | solution.py:392
  31.2 1.5 %collective-permute-start.4 = (f32[272,256]{1,0:T(8,128)S(1)}, f32[272,256]{1,0:T(8,128)S(1)}, u32[]{:S(2)}, u32[]{:S(2)}) collective-permute-start(f32[272,256]{1,0:T(8,128)S(1)} %get-tuple-element.130), channel_id=1, source_target_pairs={{0,2},{2,0},{4,6},{6,4},{8,10},{10,8},{12,14},{14,12},{1,3},{3,1},... | collective-permute-start | bytes 835592 | tf_op jit(solution)/shard_map/ppermute | solution.py:392
  32.7 3.3 %collective-permute-start.5 = (f32[272,256]{1,0:T(8,128)S(1)}, f32[272,256]{1,0:T(8,128)S(1)}, u32[]{:S(2)}, u32[]{:S(2)}) collective-permute-start(f32[272,256]{1,0:T(8,128)S(1)} %get-tuple-element.131), channel_id=1, source_target_pairs={{2,4},{4,2},{6,8},{8,6},{10,12},{12,10},{14,0},{0,14},{3,5},{5,3},... | collective-permute-start | bytes 835592 | tf_op jit(solution)/shard_map/ppermute | solution.py:392
  36.6 8.5 %collective-permute-done.4.refs_1_ = f32[272,256]{1,0:T(8,128)S(1)} collective-permute-done((f32[272,256]{1,0:T(8,128)S(1)}, f32[272,256]{1,0:T(8,128)S(1)}, u32[]{:S(2)}, u32[]{:S(2)}) %collective-permute-start.4) | collective-permute-done | bytes 278560 | tf_op jit(solution)/shard_map/ppermute | solution.py:392
  45.1 1.2 %shard_map.162 = (f32[2,3,4,40,256]{4,3,2,1,0:T(8,128)S(1)}, f32[2,3,4,40,256]{4,3,2,1,0:T(8,128)S(1)}, f32[2,3,4,40,256]{4,3,2,1,0:T(8,128)S(1)}, f32[2,3,4,40,...) custom-call(f32[4,8,256]{2,1,0:T(8,128)S(1)} %get-tuple-element.102., ...), custom_call_target="tpu_custom_call", output_to_operand_aliasing={{0}: (5, {}), {1}: (6, {}), {2}: (7, {}), {3}: (8, {}), {4}... | custom-call | tf_op jit(solution)/shard_map/pallas_call | solution.py:377
  46.3 1.3 %collective-permute-start.6 = (f32[48,8,256]{2,1,0:T(8,128)S(1)}, f32[48,8,256]{2,1,0:T(8,128)S(1)}, u32[]{:S(2)}, u32[]{:S(2)}) collective-permute-start(f32[48,8,256]{2,1,0:T(8,128)S(1)} %get-tuple-element.146), channel_id=1, source_target_pairs={{0,1},{1,0},{2,3},{3,2},{4,5},{5,4},{6,7},{7,6},{8,9},{9,8},{10,11... | collective-permute-start | bytes 1179656 | tf_op jit(solution)/shard_map/ppermute | solution.py:392
  47.5 1.3 %collective-permute-done.6.refs_1_ = f32[48,8,256]{2,1,0:T(8,128)S(1)} collective-permute-done((f32[48,8,256]{2,1,0:T(8,128)S(1)}, f32[48,8,256]{2,1,0:T(8,128)S(1)}, u32[]{:S(2)}, u32[]{:S(2)}) %collective-permute-start.6) | collective-permute-done | bytes 393248 | tf_op jit(solution)/shard_map/ppermute | solution.py:392
  49.7 1.5 %collective-permute-start.7 = (f32[272,256]{1,0:T(8,128)S(1)}, f32[272,256]{1,0:T(8,128)S(1)}, u32[]{:S(2)}, u32[]{:S(2)}) collective-permute-start(f32[272,256]{1,0:T(8,128)S(1)} %get-tuple-element.152), channel_id=1, source_target_pairs={{0,2},{2,0},{4,6},{6,4},{8,10},{10,8},{12,14},{14,12},{1,3},{3,1},... | collective-permute-start | bytes 835592 | tf_op jit(solution)/shard_map/ppermute | solution.py:392
  51.2 3.3 %collective-permute-start.8 = (f32[272,256]{1,0:T(8,128)S(1)}, f32[272,256]{1,0:T(8,128)S(1)}, u32[]{:S(2)}, u32[]{:S(2)}) collective-permute-start(f32[272,256]{1,0:T(8,128)S(1)} %get-tuple-element.153), channel_id=1, source_target_pairs={{2,4},{4,2},{6,8},{8,6},{10,12},{12,10},{14,0},{0,14},{3,5},{5,3},... | collective-permute-start | bytes 835592 | tf_op jit(solution)/shard_map/ppermute | solution.py:392
  55.0 8.5 %collective-permute-done.7.refs_1_ = f32[272,256]{1,0:T(8,128)S(1)} collective-permute-done((f32[272,256]{1,0:T(8,128)S(1)}, f32[272,256]{1,0:T(8,128)S(1)}, u32[]{:S(2)}, u32[]{:S(2)}) %collective-permute-start.7) | collective-permute-done | bytes 278560 | tf_op jit(solution)/shard_map/ppermute | solution.py:392
  63.6 1.2 %shard_map.165 = (f32[2,3,4,40,256]{4,3,2,1,0:T(8,128)S(1)}, f32[2,3,4,40,256]{4,3,2,1,0:T(8,128)S(1)}, f32[2,3,4,40,256]{4,3,2,1,0:T(8,128)S(1)}, f32[2,3,4,40,...) custom-call(f32[4,8,256]{2,1,0:T(8,128)S(1)} %get-tuple-element.102., ...), custom_call_target="tpu_custom_call", output_to_operand_aliasing={{0}: (5, {}), {1}: (6, {}), {2}: (7, {}), {3}: (8, {}), {4}... | custom-call | tf_op jit(solution)/shard_map/pallas_call | solution.py:377
  64.7 1.3 %collective-permute-start.9 = (f32[48,8,256]{2,1,0:T(8,128)S(1)}, f32[48,8,256]{2,1,0:T(8,128)S(1)}, u32[]{:S(2)}, u32[]{:S(2)}) collective-permute-start(f32[48,8,256]{2,1,0:T(8,128)S(1)} %get-tuple-element.167), channel_id=1, source_target_pairs={{0,1},{1,0},{2,3},{3,2},{4,5},{5,4},{6,7},{7,6},{8,9},{9,8},{10,11... | collective-permute-start | bytes 1179656 | tf_op jit(solution)/shard_map/ppermute | solution.py:392
  66.0 1.3 %collective-permute-done.9.refs_1_ = f32[48,8,256]{2,1,0:T(8,128)S(1)} collective-permute-done((f32[48,8,256]{2,1,0:T(8,128)S(1)}, f32[48,8,256]{2,1,0:T(8,128)S(1)}, u32[]{:S(2)}, u32[]{:S(2)}) %collective-permute-start.9) | collective-permute-done | bytes 393248 | tf_op jit(solution)/shard_map/ppermute | solution.py:392
  68.1 1.5 %collective-permute-start.10 = (f32[272,256]{1,0:T(8,128)S(1)}, f32[272,256]{1,0:T(8,128)S(1)}, u32[]{:S(2)}, u32[]{:S(2)}) collective-permute-start(f32[272,256]{1,0:T(8,128)S(1)} %get-tuple-element.173), channel_id=1, source_target_pairs={{0,2},{2,0},{4,6},{6,4},{8,10},{10,8},{12,14},{14,12},{1,3},{3,1},... | collective-permute-start | bytes 835592 | tf_op jit(solution)/shard_map/ppermute | solution.py:392
  69.7 3.3 %collective-permute-start.11 = (f32[272,256]{1,0:T(8,128)S(1)}, f32[272,256]{1,0:T(8,128)S(1)}, u32[]{:S(2)}, u32[]{:S(2)}) collective-permute-start(f32[272,256]{1,0:T(8,128)S(1)} %get-tuple-element.174), channel_id=1, source_target_pairs={{2,4},{4,2},{6,8},{8,6},{10,12},{12,10},{14,0},{0,14},{3,5},{5,3},... | collective-permute-start | bytes 835592 | tf_op jit(solution)/shard_map/ppermute | solution.py:392
  73.5 8.5 %collective-permute-done.10.refs_1_ = f32[272,256]{1,0:T(8,128)S(1)} collective-permute-done((f32[272,256]{1,0:T(8,128)S(1)}, f32[272,256]{1,0:T(8,128)S(1)}, u32[]{:S(2)}, u32[]{:S(2)}) %collective-permute-start.10) | collective-permute-done | bytes 278560 | tf_op jit(solution)/shard_map/ppermute | solution.py:392
  82.1 1.2 %shard_map.168 = (f32[2,3,4,40,256]{4,3,2,1,0:T(8,128)S(1)}, f32[2,3,4,40,256]{4,3,2,1,0:T(8,128)S(1)}, f32[2,3,4,40,256]{4,3,2,1,0:T(8,128)S(1)}, f32[2,3,4,40,...) custom-call(f32[4,8,256]{2,1,0:T(8,128)S(1)} %get-tuple-element.102., ...), custom_call_target="tpu_custom_call", output_to_operand_aliasing={{0}: (5, {}), {1}: (6, {}), {2}: (7, {}), {3}: (8, {}), {4}... | custom-call | tf_op jit(solution)/shard_map/pallas_call | solution.py:377
  83.3 1.3 %collective-permute-start.12 = (f32[2,4,8,128]{3,2,1,0:T(8,128)S(1)}, f32[2,4,8,128]{3,2,1,0:T(8,128)S(1)}, u32[]{:S(2)}, u32[]{:S(2)}) collective-permute-start(f32[2,4,8,128]{3,2,1,0:T(8,128)S(1)} %get-tuple-element.196.own), channel_id=1, source_target_pairs={{0,1},{1,0},{2,3},{3,2},{4,5},{5,4},{6,7},{7,6},{8,9},{9,8},{10,11... | collective-permute-start | bytes 98312 | tf_op jit(solution)/shard_map/ppermute | solution.py:392
  84.6 1.7 %shard_map.169 = (f32[2,3,4,32,256]{4,3,2,1,0:T(8,128)}, f32[2,3,4,32,256]{4,3,2,1,0:T(8,128)}, f32[2,3,4,32,256]{4,3,2,1,0:T(8,128)}, f32[2,3,4,32,256]{4,3,2,1,0:T(8,128)}) custom-call(f32[2,3,4,40,256]{4,3,2,1,0:T(8,128)S(1)} %get-tuple-element.188.e, f32[2,3,4,40,256]{4,3,2,1,0:T(8,128)S(1)} %get-tuple-element.189.h, ...), custom_call_target="tpu_custom_call" | custom-call | flops 4194304 | bytes 4194304 | tf_op jit(solution)/shard_map/pallas_call | solution.py:377
  (42 shorter events, 14.2 us)
Async XLA Ops:
  0.6 1.1 %copy-start = (f32[2,3,4,32,256]{4,3,2,1,0:T(8,128)S(1)}, f32[2,3,4,32,256]{4,3,2,1,0:T(8,128)}, u32[]{:S(2)}) copy-start(f32[2,3,4,32,256]{4,3,2,1,0:T(8,128)} %e_in.1) | copy-start | bytes 2359300
  1.8 1.1 %copy-start.1 = (f32[2,3,4,32,256]{4,3,2,1,0:T(8,128)S(1)}, f32[2,3,4,32,256]{4,3,2,1,0:T(8,128)}, u32[]{:S(2)}) copy-start(f32[2,3,4,32,256]{4,3,2,1,0:T(8,128)} %h_in.1) | copy-start | bytes 2359300
  2.9 1.1 %copy-start.2 = (f32[2,3,4,32,256]{4,3,2,1,0:T(8,128)S(1)}, f32[2,3,4,32,256]{4,3,2,1,0:T(8,128)}, u32[]{:S(2)}) copy-start(f32[2,3,4,32,256]{4,3,2,1,0:T(8,128)} %p_in.1) | copy-start | bytes 2359300
  4.0 1.1 %copy-start.3 = (f32[2,3,4,32,256]{4,3,2,1,0:T(8,128)S(1)}, f32[2,3,4,32,256]{4,3,2,1,0:T(8,128)}, u32[]{:S(2)}) copy-start(f32[2,3,4,32,256]{4,3,2,1,0:T(8,128)} %j_in.1) | copy-start | bytes 2359300
  5.2 0.9 %copy-start.4 = (s32[4,32,256]{2,1,0:T(8,128)S(1)}, s32[4,32,256]{2,1,0:T(8,128)}, u32[]{:S(2)}) copy-start(s32[4,32,256]{2,1,0:T(8,128)} %mat_in.1) | copy-start | bytes 393220
  6.7 0.7 copy-start.10
  6.7 0.7 copy-start.11
  6.7 0.7 copy-start.6
  6.7 0.7 copy-start.7
  6.7 0.7 copy-start.8
  6.8 1.8 %collective-permute-start = (f32[52,8,256]{2,1,0:T(8,128)S(1)}, f32[52,8,256]{2,1,0:T(8,128)S(1)}, u32[]{:S(2)}, u32[]{:S(2)}) collective-permute-start(f32[52,8,256]{2,1,0:T(8,128)S(1)} %get-tuple-element.103), channel_id=1, source_target_pairs={{0,1},{1,0},{2,3},{3,2},{4,5},{5,4},{6,7},{7,6},{8,9},{9,8},{10,11... | collective-permute-start | bytes 1277960 | tf_op jit(solution)/shard_map/ppermute | solution.py:392
  10.0 16.9 %collective-permute-start.1 = (f32[312,256]{1,0:T(8,128)S(1)}, f32[312,256]{1,0:T(8,128)S(1)}, u32[]{:S(2)}, u32[]{:S(2)}) collective-permute-start(f32[312,256]{1,0:T(8,128)S(1)} %get-tuple-element.109), channel_id=1, source_target_pairs={{0,2},{2,0},{4,6},{6,4},{8,10},{10,8},{12,14},{14,12},{1,3},{3,1},... | collective-permute-start | bytes 958472 | tf_op jit(solution)/shard_map/ppermute | solution.py:392
  12.4 14.5 %collective-permute-start.2 = (f32[312,256]{1,0:T(8,128)S(1)}, f32[312,256]{1,0:T(8,128)S(1)}, u32[]{:S(2)}, u32[]{:S(2)}) collective-permute-start(f32[312,256]{1,0:T(8,128)S(1)} %get-tuple-element.110), channel_id=1, source_target_pairs={{2,4},{4,2},{6,8},{8,6},{10,12},{12,10},{14,0},{0,14},{3,5},{5,3},... | collective-permute-start | bytes 958472 | tf_op jit(solution)/shard_map/ppermute | solution.py:392
  28.1 2.3 %collective-permute-start.3 = (f32[48,8,256]{2,1,0:T(8,128)S(1)}, f32[48,8,256]{2,1,0:T(8,128)S(1)}, u32[]{:S(2)}, u32[]{:S(2)}) collective-permute-start(f32[48,8,256]{2,1,0:T(8,128)S(1)} %get-tuple-element.124), channel_id=1, source_target_pairs={{0,1},{1,0},{2,3},{3,2},{4,5},{5,4},{6,7},{7,6},{8,9},{9,8},{10,11... | collective-permute-start | bytes 1179656 | tf_op jit(solution)/shard_map/ppermute | solution.py:392
  31.2 13.9 %collective-permute-start.4 = (f32[272,256]{1,0:T(8,128)S(1)}, f32[272,256]{1,0:T(8,128)S(1)}, u32[]{:S(2)}, u32[]{:S(2)}) collective-permute-start(f32[272,256]{1,0:T(8,128)S(1)} %get-tuple-element.130), channel_id=1, source_target_pairs={{0,2},{2,0},{4,6},{6,4},{8,10},{10,8},{12,14},{14,12},{1,3},{3,1},... | collective-permute-start | bytes 835592 | tf_op jit(solution)/shard_map/ppermute | solution.py:392
  32.7 12.4 %collective-permute-start.5 = (f32[272,256]{1,0:T(8,128)S(1)}, f32[272,256]{1,0:T(8,128)S(1)}, u32[]{:S(2)}, u32[]{:S(2)}) collective-permute-start(f32[272,256]{1,0:T(8,128)S(1)} %get-tuple-element.131), channel_id=1, source_target_pairs={{2,4},{4,2},{6,8},{8,6},{10,12},{12,10},{14,0},{0,14},{3,5},{5,3},... | collective-permute-start | bytes 835592 | tf_op jit(solution)/shard_map/ppermute | solution.py:392
  46.3 2.6 %collective-permute-start.6 = (f32[48,8,256]{2,1,0:T(8,128)S(1)}, f32[48,8,256]{2,1,0:T(8,128)S(1)}, u32[]{:S(2)}, u32[]{:S(2)}) collective-permute-start(f32[48,8,256]{2,1,0:T(8,128)S(1)} %get-tuple-element.146), channel_id=1, source_target_pairs={{0,1},{1,0},{2,3},{3,2},{4,5},{5,4},{6,7},{7,6},{8,9},{9,8},{10,11... | collective-permute-start | bytes 1179656 | tf_op jit(solution)/shard_map/ppermute | solution.py:392
  49.7 13.9 %collective-permute-start.7 = (f32[272,256]{1,0:T(8,128)S(1)}, f32[272,256]{1,0:T(8,128)S(1)}, u32[]{:S(2)}, u32[]{:S(2)}) collective-permute-start(f32[272,256]{1,0:T(8,128)S(1)} %get-tuple-element.152), channel_id=1, source_target_pairs={{0,2},{2,0},{4,6},{6,4},{8,10},{10,8},{12,14},{14,12},{1,3},{3,1},... | collective-permute-start | bytes 835592 | tf_op jit(solution)/shard_map/ppermute | solution.py:392
  51.2 12.4 %collective-permute-start.8 = (f32[272,256]{1,0:T(8,128)S(1)}, f32[272,256]{1,0:T(8,128)S(1)}, u32[]{:S(2)}, u32[]{:S(2)}) collective-permute-start(f32[272,256]{1,0:T(8,128)S(1)} %get-tuple-element.153), channel_id=1, source_target_pairs={{2,4},{4,2},{6,8},{8,6},{10,12},{12,10},{14,0},{0,14},{3,5},{5,3},... | collective-permute-start | bytes 835592 | tf_op jit(solution)/shard_map/ppermute | solution.py:392
  64.7 2.6 %collective-permute-start.9 = (f32[48,8,256]{2,1,0:T(8,128)S(1)}, f32[48,8,256]{2,1,0:T(8,128)S(1)}, u32[]{:S(2)}, u32[]{:S(2)}) collective-permute-start(f32[48,8,256]{2,1,0:T(8,128)S(1)} %get-tuple-element.167), channel_id=1, source_target_pairs={{0,1},{1,0},{2,3},{3,2},{4,5},{5,4},{6,7},{7,6},{8,9},{9,8},{10,11... | collective-permute-start | bytes 1179656 | tf_op jit(solution)/shard_map/ppermute | solution.py:392
  68.1 13.9 %collective-permute-start.10 = (f32[272,256]{1,0:T(8,128)S(1)}, f32[272,256]{1,0:T(8,128)S(1)}, u32[]{:S(2)}, u32[]{:S(2)}) collective-permute-start(f32[272,256]{1,0:T(8,128)S(1)} %get-tuple-element.173), channel_id=1, source_target_pairs={{0,2},{2,0},{4,6},{6,4},{8,10},{10,8},{12,14},{14,12},{1,3},{3,1},... | collective-permute-start | bytes 835592 | tf_op jit(solution)/shard_map/ppermute | solution.py:392
  69.7 12.4 %collective-permute-start.11 = (f32[272,256]{1,0:T(8,128)S(1)}, f32[272,256]{1,0:T(8,128)S(1)}, u32[]{:S(2)}, u32[]{:S(2)}) collective-permute-start(f32[272,256]{1,0:T(8,128)S(1)} %get-tuple-element.174), channel_id=1, source_target_pairs={{2,4},{4,2},{6,8},{8,6},{10,12},{12,10},{14,0},{0,14},{3,5},{5,3},... | collective-permute-start | bytes 835592 | tf_op jit(solution)/shard_map/ppermute | solution.py:392
  72.9 9.1 %copy-start.5 = (f32[2,16,32]{2,1,0:T(8,128)S(1)}, f32[2,16,32]{2,1,0:T(8,128)}, u32[]{:S(2)}) copy-start(f32[2,16,32]{2,1,0:T(8,128)} %constant.2.clone.refs_11_) | copy-start | bytes 12292
  83.3 3.0 %collective-permute-start.12 = (f32[2,4,8,128]{3,2,1,0:T(8,128)S(1)}, f32[2,4,8,128]{3,2,1,0:T(8,128)S(1)}, u32[]{:S(2)}, u32[]{:S(2)}) collective-permute-start(f32[2,4,8,128]{3,2,1,0:T(8,128)S(1)} %get-tuple-element.196.own), channel_id=1, source_target_pairs={{0,1},{1,0},{2,3},{3,2},{4,5},{5,4},{6,7},{7,6},{8,9},{9,8},{10,11... | collective-permute-start | bytes 98312 | tf_op jit(solution)/shard_map/ppermute | solution.py:392
  (1 other events, 0.7 us)

commit v2 on v1

v2 whole, which is shorter than its diff:
```python
import functools
import math

import jax
import jax.numpy as jnp
import numpy as np
from jax import lax
from jax.experimental import pallas as pl
from jax.experimental.pallas import tpu as pltpu
from jax.sharding import PartitionSpec as P

STEPS = 8
HARM = 8
EDGE = 8
ORDER = (0, 1)
courant = 0.5
VMEM_LIMIT = 8 << 20


def next_y(v):
    return pltpu.roll(v, v.shape[0] - 1, 0)


def prev_y(v):
    return pltpu.roll(v, 1, 0)


def next_z(v):
    lane = lax.broadcasted_iota(jnp.int32, v.shape, 1)
    return jnp.where(lane == v.shape[1] - 1, 0.0, pltpu.roll(v, v.shape[1] - 1, 1))


def prev_z(v):
    lane = lax.broadcasted_iota(jnp.int32, v.shape, 1)
    return jnp.where(lane == 0, 0.0, pltpu.roll(v, 1, 1))


def turn(pair, cos_v, sin_v):
    return cos_v * pair[0] - sin_v * pair[1], sin_v * pair[0] + cos_v * pair[1]


def sublane(v):
    return lax.broadcasted_iota(jnp.int32, v.shape, 0)


def weave(first, second):
    row = sublane(first)
    return jnp.where((row < 2) | (row >= 6), first, pltpu.roll(second, 4, 0))


def edge_rows(ref, at, rows):
    low = ref[at + (slice(0, 8),)]
    high = ref[at + (slice(rows - 8, rows),)]
    return jnp.where(sublane(low) < 4, low, high)


def pack_edges(fields, out, rows, xs):
    e, h, p, j = fields
    for r in range(2):
        for g, (one, two) in enumerate(((e, h), (p, j))):
            for k in range(3):
                for i, x in enumerate(xs):
                    at = (r, k, x)
                    tile = weave(edge_rows(one, at, rows), edge_rows(two, at, rows))
                    out[((r * 2 + g) * 3 + k) * len(xs) + i] = tile


def wrap_phase(cs, axis, name, up):
    at, count = lax.axis_index(name), lax.axis_size(name)
    wraps = at == (count - 1 if up else 0)
    sine = cs[2 + axis, 0:1]
    return jnp.where(wraps, cs[axis, 0:1], 1.0), jnp.where(wraps, sine if up else 0.0 - sine, 0.0)


def unpack_edges(recv, fields, cs, rows, xs):
    e, h, p, j = fields
    up, dn = wrap_phase(cs, 1, "gy", True), wrap_phase(cs, 1, "gy", False)
    depth = e.shape[4]
    row = lax.broadcasted_iota(jnp.int32, (8, depth), 0)
    cos_v = jnp.where(row < 4, up[0], dn[0])
    sin_v = jnp.where(row < 4, up[1], dn[1])
    for g, (one, two) in enumerate(((e, h), (p, j))):
        for k in range(3):
            for i, x in enumerate(xs):
                pair = [recv[((r * 2 + g) * 3 + k) * len(xs) + i] for r in range(2)]
                for dst in (one, two):
                    re, im = turn(pair, cos_v, sin_v)
                    dst[0, k, x, rows:] = re
                    dst[1, k, x, rows:] = im
                    pair = [pltpu.roll(v, 4, 0) for v in pair]


def curl_e_x(ey, ez):
    return (next_y(ez) - ez) - (next_z(ey) - ey)


def magnetic_full(e, h, r, x, nxt):
    ex, ey, ez = (e[r, k, x] for k in range(3))
    ny_, nz_ = nxt
    h[r, 0, x] = h[r, 0, x] - courant * curl_e_x(ey, ez)
    h[r, 1, x] = h[r, 1, x] - courant * ((next_z(ex) - ex) - (nz_ - ez))
    h[r, 2, x] = h[r, 2, x] - courant * ((ny_ - ey) - (next_y(ex) - ex))


def magnetic_open(ex, ey, ez, hy, hz):
    hy = hy - courant * ((next_z(ex) - ex) + ez)
    hz = hz - courant * ((0.0 - ey) - (next_y(ex) - ex))
    return hy, hz


def polarize_step(e, p, j, coef, r, x):
    for k in range(3):
        now = coef[1, x] * j[r, k, x] + coef[2, x] * (coef[3, x] * e[r, k, x] - p[r, k, x])
        j[r, k, x] = now
        p[r, k, x] = p[r, k, x] + courant * now


def electric_step(e, h, j, coef, r, x, prev):
    hx, hy, hz = (h[r, k, x] for k in range(3))
    inv = coef[0, x]
    e[r, 0, x] = e[r, 0, x] + inv * ((hz - prev_y(hz)) - (hy - prev_z(hy)) - j[r, 0, x])
    dz, dy = hz, hy
    if prev is not None:
        dz, dy = hz - prev[1], hy - prev[0]
    e[r, 1, x] = e[r, 1, x] + inv * ((hx - prev_z(hx)) - dz - j[r, 1, x])
    e[r, 2, x] = e[r, 2, x] + inv * (dy - (hx - prev_y(hx)) - j[r, 2, x])


def response(inv, dhy, dhz):
    dex = inv * ((dhz - prev_y(dhz)) - (dhy - prev_z(dhy)))
    return dex, 0.0 - inv * dhz, inv * dhy


def note_top(e, rec, r, x, step, rows):
    depth = e.shape[4]
    top = e[r, 0, x, 0:rows, depth - 128 :]
    lane = lax.broadcasted_iota(jnp.int32, top.shape, 1)
    rec[r, x] = jnp.where(lane == step, pltpu.roll(top, (step + 1) % 128, 1), rec[r, x])


def start_body(rows, e_in, h_in, p_in, j_in, mat_in, e, h, p, j, mat, edges, sems):
    pairs = [(src, dst.at[:, :, :, 0:rows]) for src, dst in ((e_in, e), (h_in, h), (p_in, p), (j_in, j))]
    copies = [pltpu.make_async_copy(src, dst, sems.at[i]) for i, (src, dst) in enumerate(pairs + [(mat_in, mat)])]
    for c in copies:
        c.start()
    for dst in (e, h, p, j):
        dst[:, :, :, rows:] = jnp.zeros(dst.shape[:3] + (EDGE, dst.shape[4]), jnp.float32)
    for c in copies:
        c.wait()
    pack_edges((e, h, p, j), edges, rows, range(e.shape[2]))
    base = 2 * 2 * 3 * e.shape[2]
    for x in range(e.shape[2]):
        edges[base + x] = edge_rows(mat, (x,), rows).astype(jnp.float32)


def store_body(rows, e, h, p, j, e_out, h_out, p_out, j_out, sems):
    pairs = ((e, e_out), (h, h_out), (p, p_out), (j, j_out))
    copies = [
        pltpu.make_async_copy(src.at[:, :, :, 0:rows], dst, sems.at[i]) for i, (src, dst) in enumerate(pairs)
    ]
    for c in copies:
        c.start()
    for c in copies:
        c.wait()


def panel_body(own, other, out):
    for r in range(2):
        for x in range(own.shape[1]):
            out[r, :, x] = jnp.transpose(own[r, x] + other[r, x])[0:STEPS]


def cell_tables(kind, pole_of, eps, dec, frq, stg):
    vals = [jnp.full(kind.shape, t, jnp.float32) for t in (eps[0], dec[pole_of[0]], frq[pole_of[0]], stg[pole_of[0]])]
    for m in range(1, eps.shape[0]):
        hit = kind == m
        pole = pole_of[m]
        for i, t in enumerate((eps[m], dec[pole], frq[pole], stg[pole])):
            vals[i] = jnp.where(hit, t, vals[i])
    vals[0] = courant / vals[0]
    return vals


def coef_body(rows, mat, pole_of, eps, dec, frq, stg, bloch, coef, cs, rec):
    rec[...] = jnp.zeros(rec.shape, jnp.float32)
    for i in range(2):
        turns = jnp.full(cs.shape[1:], bloch[i], jnp.float32)
        cs[i] = jnp.cos(turns)
        cs[2 + i] = jnp.sin(turns)
    for x in range(mat.shape[0]):
        for y in range(0, rows, 8):
            vals = cell_tables(mat[x, y : y + 8], pole_of, eps, dec, frq, stg)
            for i in range(4):
                coef[i, x, y : y + 8] = vals[i]
        for i in range(4):
            coef[i, x, rows:] = jnp.zeros((EDGE, coef.shape[3]), jnp.float32)


def by_side(which, upper, lower):
    mine = lax.axis_index("gx") % 2 == which
    pl.when(mine)(upper)
    pl.when(jnp.logical_not(mine))(lower)


def send_body(rows, which, first, step, refs):
    refs = list(refs)
    second = which == ORDER[1]
    if second:
        rec = refs.pop()
        refs.pop(5 if first else 7)
    if first and which == ORDER[0]:
        cs, edges, pole_of, eps, dec, frq, stg = refs[0:7]
        e, h, p, j, coef, e0, out = refs[12:]
    elif first:
        e, h, p, j, e0, out = refs[5:]
        coef = refs[4]
    else:
        cs, edges = refs[0:2]
        coef = refs[6]
        e, h, p, j, e0, out = refs[7:]
    planes = e.shape[2]
    last = planes - 1
    half = 4 * rows
    if first and which == ORDER[0]:
        unpack_edges(edges, (e, h, p, j), cs, rows, range(planes))
        base = 2 * 2 * 3 * planes
        for x in range(planes):
            kind = edges[base + x].astype(jnp.int32)
            vals = cell_tables(kind, pole_of, eps, dec, frq, stg)
            for i in range(4):
                coef[i, x, rows:] = vals[i]

    def upper():
        if not first:
            unpack_edges(edges, (e, h, p, j), cs, rows, (last - 1, last))
        for r in range(2):
            tiles = []
            magnetic_full(e, h, r, last - 1, (e[r, 1, last], e[r, 2, last]))
            ex, ey, ez = (e[r, k, last] for k in range(3))
            h[r, 0, last] = h[r, 0, last] - courant * curl_e_x(ey, ez)
            hs = magnetic_open(ex, ey, ez, h[r, 1, last], h[r, 2, last])
            for k in range(2):
                h[r, 1 + k, last] = hs[k]
                out[(2 * r + k) * rows : (2 * r + k + 1) * rows] = hs[k][0:rows]
                tiles.append(hs[k][rows:])
            polarize_step(e, p, j, coef, r, last)
            electric_step(e, h, j, coef, r, last, (h[r, 1, last - 1], h[r, 2, last - 1]))
            ex, ey, ez = (e[r, k, last] for k in range(3))
            hs = magnetic_open(ex, ey, ez, h[r, 1, last], h[r, 2, last])
            for k in range(2):
                at = half + (2 * r + k) * rows
                out[at : at + rows] = hs[k][0:rows]
            at = 2 * half + 8 * r
            out[at : at + 8] = weave(*tiles)
        if first:
            out[2 * half + 16 :] = coef[0, last]

    def lower():
        if not first:
            unpack_edges(edges, (e, h, p, j), cs, rows, (0, 1))
        for r in range(2):
            tiles = []
            magnetic_full(e, h, r, 0, (e[r, 1, 1], e[r, 2, 1]))
            for k in range(2):
                now = e[r, 1 + k, 0]
                e0[r, k] = now
                out[(2 * r + k) * rows : (2 * r + k + 1) * rows] = now[0:rows]
                tiles.append(now[rows:])
            polarize_step(e, p, j, coef, r, 0)
            electric_step(e, h, j, coef, r, 0, None)
            for k in range(2):
                at = half + (2 * r + k) * rows
                now = e[r, 1 + k, 0]
                out[at : at + rows] = now[0:rows]
                row = sublane(tiles[k])
                tiles[k] = jnp.where(row == 1, pltpu.roll(now[rows:], 2, 0), tiles[k])
            at = 2 * half + 8 * r
            out[at : at + 8] = weave(*tiles)
        if first:
            out[2 * half + 16 :] = coef[0, 0]

    by_side(which, upper, lower)
    if second:
        inner_part(rows, step, (e, h, p, j, rec), coef)


def inner_part(rows, step, state, coef):
    e, h, p, j, rec = state
    planes = e.shape[2]
    for r in range(2):
        for x in range(1, planes - 2):
            magnetic_full(e, h, r, x, (e[r, 1, x + 1], e[r, 2, x + 1]))
        for x in range(1, planes - 1):
            polarize_step(e, p, j, coef, r, x)
            electric_step(e, h, j, coef, r, x, (h[r, 1, x - 1], h[r, 2, x - 1]))
        for x in range(planes - 1):
            note_top(e, rec, r, x, step, rows)
        for x in range(1, planes - 2):
            magnetic_full(e, h, r, x, (e[r, 1, x + 1], e[r, 2, x + 1]))
        for x in range(1, planes - 1):
            polarize_step(e, p, j, coef, r, x)


def finish_body(rows, which, step, final, refs):
    cs, msg, e0, far, coef = refs[0:5]
    refs = refs[10:]
    e, h, p, j, rec = refs[0:5]
    planes = e.shape[2]
    last = planes - 1
    half = 4 * rows
    inv_far = far[2 * half + 16 : 2 * half + 16 + rows + EDGE]

    def arrived(cos_v, sin_v):
        res = []
        for k in range(2):
            raw = []
            for r in range(2):
                tile = msg[2 * half + 8 * r : 2 * half + 8 * r + 8]
                if k == 1:
                    tile = pltpu.roll(tile, 4, 0)
                at = (2 * r + k) * rows
                one = jnp.concatenate([msg[at : at + rows], tile], axis=0)
                two = jnp.concatenate([msg[half + at : half + at + rows], pltpu.roll(tile, 6, 0)], axis=0)
                raw.append((one, two))
            res.append((turn((raw[0][0], raw[1][0]), cos_v, sin_v), turn((raw[0][1], raw[1][1]), cos_v, sin_v)))
        return res

    def upper():
        above = arrived(*wrap_phase(cs, 0, "gx", True))
        for r in range(2):
            a0y, a0z = above[0][0][r], above[1][0][r]
            dhy, dhz = courant * a0z, 0.0 - courant * a0y
            hy = h[r, 1, last] + dhy
            hz = h[r, 2, last] + dhz
            h[r, 1, last] = hy
            h[r, 2, last] = hz
            for k, d in enumerate(response(coef[0, last], dhy, dhz)):
                e[r, k, last] = e[r, k, last] + d
            note_top(e, rec, r, last, step, rows)
            a1y = above[0][1][r] + inv_far * hz
            a1z = above[1][1][r] - inv_far * hy
            magnetic_full(e, h, r, last - 1, (e[r, 1, last], e[r, 2, last]))
            magnetic_full(e, h, r, last, (a1y, a1z))
            polarize_step(e, p, j, coef, r, last)
            for x in (last - 1, last):
                electric_step(e, h, j, coef, r, x, (h[r, 1, x - 1], h[r, 2, x - 1]))
                note_top(e, rec, r, x, step + 1, rows)
        if not final:
            pack_edges((e, h, p, j), refs[5], rows, (last - 1, last))

    def lower():
        below = arrived(*wrap_phase(cs, 0, "gx", False))
        for r in range(2):
            dhy, dhz = courant * e0[r, 1], 0.0 - courant * e0[r, 0]
            e[r, 1, 0] = e[r, 1, 0] + coef[0, 0] * (below[1][0][r] + dhz)
            e[r, 2, 0] = e[r, 2, 0] - coef[0, 0] * (below[0][0][r] + dhy)
            dex, dey, dez = response(inv_far, dhy, dhz)
            hy, hz = magnetic_open(dex, dey, dez, dhy, dhz)
            b1y = below[0][1][r] + hy + courant * e[r, 2, 0]
            b1z = below[1][1][r] + hz - courant * e[r, 1, 0]
            magnetic_full(e, h, r, 0, (e[r, 1, 1], e[r, 2, 1]))
            polarize_step(e, p, j, coef, r, 0)
            electric_step(e, h, j, coef, r, 0, (b1y, b1z))
            electric_step(e, h, j, coef, r, 1, (h[r, 1, 0], h[r, 2, 0]))
            for x in range(2):
                note_top(e, rec, r, x, step + 1, rows)
        if not final:
            pack_edges((e, h, p, j), refs[5], rows, (0, 1))

    by_side(which, upper, lower)


def harmonics_body(rec, waves, harm):
    wave = waves[lax.axis_index("gy")]
    for x in range(rec.shape[1]):
        re, im = (
            jnp.dot(wave, rec[r, x], precision=lax.Precision.HIGHEST, preferred_element_type=jnp.float32)
            for r in range(2)
        )
        harm[0, x] = re[0:HARM] + im[HARM:]
        harm[1, x] = im[0:HARM] - re[HARM:]


def call(body, ins, outs, aliases=None, smem=(), hbm_in=(), hbm_out=False, scratch=(), cost=0):
    shapes = [jax.ShapeDtypeStruct(s, d) for s, d in outs]
    ins = [pltpu.with_memory_space_constraint(v, pltpu.HBM) if i in hbm_in else v for i, v in enumerate(ins)]
    vm = pl.BlockSpec(memory_space=pltpu.VMEM)
    sm = pl.BlockSpec(memory_space=pltpu.SMEM)
    hbm = pl.BlockSpec(memory_space=pltpu.HBM)
    return pl.pallas_call(
        body,
        out_shape=shapes,
        in_specs=[sm if i in smem else hbm if i in hbm_in else vm for i in range(len(ins))],
        out_specs=[hbm if hbm_out else vm] * len(outs),
        input_output_aliases=aliases or {},
        scratch_shapes=list(scratch),
        cost_estimate=pl.CostEstimate(flops=cost, bytes_accessed=cost, transcendentals=0),
        compiler_params=pltpu.CompilerParams(vmem_limit_bytes=VMEM_LIMIT),
    )(*ins)


def swap(block, axis, shift):
    count = lax.axis_size(axis)
    pairs = [(i % count, (i + 1) % count) for i in range(shift, count, 2)]
    return lax.ppermute(block, axis, [q for a, b in pairs for q in ((a, b), (b, a))])


def per_device(
    electric, magnetic, polarize, currents, material, pole_of, eps_inf, pole_decay, pole_freq, pole_strength, bloch
):
    parts, comps, planes, rows, depth = electric.shape
    count_x, count_y = lax.axis_size("gx"), lax.axis_size("gy")
    assert count_x % 2 == 0 and count_y == 2 and planes == 4
    width_y = rows * count_y
    f32 = jnp.float32
    ext = (rows + EDGE, depth)
    angle = 2.0 * math.pi / width_y * (np.arange(HARM)[:, None] * np.arange(width_y)[None, :] % width_y)
    waves = np.concatenate([np.cos(angle), np.sin(angle)]) / math.sqrt(width_y)
    waves = jnp.asarray(np.stack(np.split(waves, count_y, axis=1)).astype(np.float32))

    state_shape = ((parts, comps, planes) + ext, f32)
    coef_shape = ((4, planes) + ext, f32)
    tiles = 2 * 2 * comps * planes
    e, h, p, j, mat, edges = call(
        functools.partial(start_body, rows),
        (electric, magnetic, polarize, currents, material),
        [state_shape] * 4 + [(material.shape, material.dtype), ((tiles + planes, 8, depth), f32)],
        hbm_in=range(5),
        scratch=[pltpu.SemaphoreType.DMA((5,))],
    )
    tables = (pole_of, eps_inf, pole_decay, pole_freq, pole_strength)
    coef, cs, rec = call(
        functools.partial(coef_body, rows),
        (mat,) + tables + (bloch,),
        [coef_shape, ((4, 8, depth), f32), ((2, planes, rows, 128), f32)],
        smem=range(1, 7),
        cost=1 << 20,
    )
    far = [None, None]
    e0 = [None, None]
    msg = [None, None]
    state = (e, h, p, j)
    keep = [state_shape] * 4
    e0_shape = ((2, 2) + ext, f32)
    side_edges = swap(edges, "gy", 0)
    size = 8 * rows + 16
    rec_shape = (rec.shape, f32)
    for which in ORDER:
        if which == ORDER[0]:
            ins = (cs, side_edges) + tables + state + (coef,)
            *state, coef, e0[which], out = call(
                lambda *refs, which=which: send_body(rows, which, True, 0, refs),
                ins,
                keep + [coef_shape, e0_shape, ((size + rows + EDGE, depth), f32)],
                {7 + i: i for i in range(5)},
                smem=range(2, 7),
            )
        else:
            *state, e0[which], out, rec = call(
                lambda *refs, which=which: send_body(rows, which, True, 0, refs),
                tuple(state) + (coef, rec),
                keep + [e0_shape, ((size + rows + EDGE, depth), f32), rec_shape],
                {0: 0, 1: 1, 2: 2, 3: 3, 5: 6},
            )
        msg[which] = far[which] = swap(out, "gx", which)
    for step in range(0, STEPS, 2):
        final = step == STEPS - 2
        for which in ORDER:
            edge_shape = [] if final else [((tiles // 2, 8, depth), f32)]
            *state, rec = call(
                lambda *refs, which=which, step=step, final=final: finish_body(rows, which, step, final, refs),
                (cs, msg[which], e0[which], far[which], coef) + tuple(state) + (rec,),
                keep + [rec_shape] + edge_shape,
                {5 + i: i for i in range(5)},
            )
            if final:
                continue
            side_edges = swap(rec, "gy", 0)
            rec = state.pop()
            second = which == ORDER[1]
            *state, e0[which], out = call(
                lambda *refs, which=which, step=step: send_body(rows, which, False, step + 2, refs),
                (cs, side_edges) + tuple(state) + (coef,) + ((rec,) if second else ()),
                keep + [e0_shape, ((size, depth), f32)] + ([rec_shape] if second else []),
                {2: 0, 3: 1, 4: 2, 5: 3, **({7: 6} if second else {})},
            )
            if second:
                rec, out = out, e0[which]
                e0[which] = state.pop()
            msg[which] = swap(out, "gx", which)
    e, h, p, j = state
    (harm,) = call(harmonics_body, (rec, waves), [((2, planes, HARM, 128), f32)])
    other = swap(harm, "gy", 0)
    fields = call(
        functools.partial(store_body, rows),
        (e, h, p, j),
        [(electric.shape, f32)] * 4,
        hbm_out=True,
        scratch=[pltpu.SemaphoreType.DMA((4,))],
        cost=1 << 22,
    )
    (panel,) = call(panel_body, (harm, other), [((2, STEPS, planes, HARM), f32)])
    return (*fields, jnp.transpose(panel, (0, 1, 3, 2)))


def solution(mesh):
    field = P("angle", None, "gx", "gy", None)
    in_specs = (field,) * 4 + (P("gx", "gy", None),) + (P(),) * 5 + (P("angle"),)
    out_specs = (field,) * 4 + (P("angle", None, None, "gx"),)
    return jax.shard_map(per_device, mesh=mesh, in_specs=in_specs, out_specs=out_specs, check_vma=False)
```

time: 87.3 us -> 79.8 us (0.914)
  waiting for transfers between devices: 40.6 us -> 32.9 us
  local copies, waits for them, and re-layouts: 6 us -> 0.73 us
  starting transfers between devices: 24.9 us -> 29.4 us
  Pallas kernels: 14.7 us -> 15.8 us
    ppermute x13 -> x16, waiting for transfers between devices: 40.6 us -> 32.9 us  [swap(): lax.ppermute(block, axis, [q for a, b in pairs for q in ((a, b), (b, a))])]
    unnamed x24 -> x14, local copies, waits for them, and re-layouts: 6 us -> 0.73 us
    ppermute x13 -> x16, starting transfers between devices: 24.9 us -> 29.4 us  [swap(): lax.ppermute(block, axis, [q for a, b in pairs for q in ((a, b), (b, a))])]
    pallas_call x16 -> x21, Pallas kernels: 14.7 us -> 15.8 us  [call(): pl.pallas_call(body, out_shape=shapes, in_specs=[sm if i in smem else hbm...]
  transfers between devices with their start and end apart: 13 -> 16, of which waited for: 8 -> 10; matrix products, arithmetic and copies ran while one was open for 0% -> 0% of each run, Pallas kernels for 6% -> 13%
where the time goes in v2:
time: 79.8 us; the launch traced here: 79.6 us
  waiting for transfers between devices  32.9 us (41%)
  starting transfers between devices  29.4 us (37%)
  Pallas kernels  15.8 us (20%)
  between operations  0.85 us (1%)
    ppermute x16, waiting for transfers between devices, swap(): lax.ppermute(block, axis, [q for a, b in pairs for q in ((a, b), (b, a))])  32.9 us
    ppermute x16, starting transfers between devices, swap(): lax.ppermute(block, axis, [q for a, b in pairs for q in ((a, b), (b, a))])  29.4 us
    pallas_call x21, Pallas kernels, call(): pl.pallas_call(body, out_shape=shapes, in_specs=[sm if i in smem else hbm...  15.8 us
  transfers between devices with their start and end apart: 16, of which 10 were waited for; matrix products, arithmetic and copies ran while one was open for 0% of the time, Pallas kernels for 13%

profile of v2, /device:TPU:1, one launch (start us, length us, event | category | flops | bytes accessed | tf_op | source)
XLA Modules:
  0.0 79.6 jit_solution(4737943461241530997)
XLA Ops:
  0.6 2.0 %shard_map.155 = (f32[2,3,4,40,256]{4,3,2,1,0:T(8,128)S(1)}, f32[2,3,4,40,256]{4,3,2,1,0:T(8,128)S(1)}, f32[2,3,4,40,256]{4,3,2,1,0:T(8,128)S(1)}, f32[2,3,4,40,...) custom-call(f32[2,3,4,32,256]{4,3,2,1,0:T(8,128)} %e_in.1, f32[2,3,4,32,256]{4,3,2,1,0:T(8,128)} %h_in.1, ...), custom_call_target="tpu_custom_call" | custom-call | tf_op jit(solution)/shard_map/pallas_call | solution.py:390
  4.5 1.1 %shard_map.157 = (f32[2,3,4,40,256]{4,3,2,1,0:T(8,128)S(1)}, f32[2,3,4,40,256]{4,3,2,1,0:T(8,128)S(1)}, f32[2,3,4,40,256]{4,3,2,1,0:T(8,128)S(1)}, f32[2,3,4,40,...) custom-call(f32[4,8,256]{2,1,0:T(8,128)S(1)} %get-tuple-element.118., ...), custom_call_target="tpu_custom_call", output_to_operand_aliasing={{0}: (7, {}), {1}: (8, {}), {2}: (9, {}), {3}: (10, {}), {4... | custom-call | tf_op jit(solution)/shard_map/pallas_call | solution.py:390
  5.6 2.3 %collective-permute-start.2 = (f32[312,256]{1,0:T(8,128)S(1)}, f32[312,256]{1,0:T(8,128)S(1)}, u32[]{:S(2)}, u32[]{:S(2)}) collective-permute-start(f32[312,256]{1,0:T(8,128)S(1)} %get-tuple-element.133), channel_id=1, source_target_pairs={{0,2},{2,0},{4,6},{6,4},{8,10},{10,8},{12,14},{14,12},{1,3},{3,1},... | collective-permute-start | bytes 958472 | tf_op jit(solution)/shard_map/ppermute | solution.py:405
  8.8 3.6 %collective-permute-start.1 = (f32[312,256]{1,0:T(8,128)S(1)}, f32[312,256]{1,0:T(8,128)S(1)}, u32[]{:S(2)}, u32[]{:S(2)}) collective-permute-start(f32[312,256]{1,0:T(8,128)S(1)} %get-tuple-element.131), channel_id=1, source_target_pairs={{2,4},{4,2},{6,8},{8,6},{10,12},{12,10},{14,0},{0,14},{3,5},{5,3},... | collective-permute-start | bytes 958472 | tf_op jit(solution)/shard_map/ppermute | solution.py:405
  12.3 10.1 %collective-permute-done.2.refs_1_.refs_3_ = f32[312,256]{1,0:T(8,128)S(1)} collective-permute-done((f32[312,256]{1,0:T(8,128)S(1)}, f32[312,256]{1,0:T(8,128)S(1)}, u32[]{:S(2)}, u32[]{:S(2)}) %collective-permute-start.2) | collective-permute-done | bytes 319520 | tf_op jit(solution)/shard_map/ppermute | solution.py:405
  23.0 0.9 %collective-permute-start.3 = (f32[24,8,256]{2,1,0:T(8,128)S(1)}, f32[24,8,256]{2,1,0:T(8,128)S(1)}, u32[]{:S(2)}, u32[]{:S(2)}) collective-permute-start(f32[24,8,256]{2,1,0:T(8,128)S(1)} %get-tuple-element.140), channel_id=1, source_target_pairs={{0,1},{1,0},{2,3},{3,2},{4,5},{5,4},{6,7},{7,6},{8,9},{9,8},{10,11... | collective-permute-start | bytes 589832 | tf_op jit(solution)/shard_map/ppermute | solution.py:405
  23.9 1.1 %collective-permute-done.3.refs_1_ = f32[24,8,256]{2,1,0:T(8,128)S(1)} collective-permute-done((f32[24,8,256]{2,1,0:T(8,128)S(1)}, f32[24,8,256]{2,1,0:T(8,128)S(1)}, u32[]{:S(2)}, u32[]{:S(2)}) %collective-permute-start.3) | collective-permute-done | bytes 196640 | tf_op jit(solution)/shard_map/ppermute | solution.py:405
  25.4 1.4 %collective-permute-start.6 = (f32[272,256]{1,0:T(8,128)S(1)}, f32[272,256]{1,0:T(8,128)S(1)}, u32[]{:S(2)}, u32[]{:S(2)}) collective-permute-start(f32[272,256]{1,0:T(8,128)S(1)} %get-tuple-element.158), channel_id=1, source_target_pairs={{0,2},{2,0},{4,6},{6,4},{8,10},{10,8},{12,14},{14,12},{1,3},{3,1},... | collective-permute-start | bytes 835592 | tf_op jit(solution)/shard_map/ppermute | solution.py:405
  28.1 1.1 %collective-permute-done.4.refs_1_ = f32[24,8,256]{2,1,0:T(8,128)S(1)} collective-permute-done((f32[24,8,256]{2,1,0:T(8,128)S(1)}, f32[24,8,256]{2,1,0:T(8,128)S(1)}, u32[]{:S(2)}, u32[]{:S(2)}) %collective-permute-start.4) | collective-permute-done | bytes 196640 | tf_op jit(solution)/shard_map/ppermute | solution.py:405
  30.1 3.7 %collective-permute-start.5 = (f32[272,256]{1,0:T(8,128)S(1)}, f32[272,256]{1,0:T(8,128)S(1)}, u32[]{:S(2)}, u32[]{:S(2)}) collective-permute-start(f32[272,256]{1,0:T(8,128)S(1)} %get-tuple-element.156), channel_id=1, source_target_pairs={{2,4},{4,2},{6,8},{8,6},{10,12},{12,10},{14,0},{0,14},{3,5},{5,3},... | collective-permute-start | bytes 835592 | tf_op jit(solution)/shard_map/ppermute | solution.py:405
  33.8 4.6 %collective-permute-done.6.refs_1_ = f32[272,256]{1,0:T(8,128)S(1)} collective-permute-done((f32[272,256]{1,0:T(8,128)S(1)}, f32[272,256]{1,0:T(8,128)S(1)}, u32[]{:S(2)}, u32[]{:S(2)}) %collective-permute-start.6) | collective-permute-done | bytes 278560 | tf_op jit(solution)/shard_map/ppermute | solution.py:405
  38.9 1.4 %collective-permute-start.7 = (f32[24,8,256]{2,1,0:T(8,128)S(1)}, f32[24,8,256]{2,1,0:T(8,128)S(1)}, u32[]{:S(2)}, u32[]{:S(2)}) collective-permute-start(f32[24,8,256]{2,1,0:T(8,128)S(1)} %get-tuple-element.165), channel_id=1, source_target_pairs={{0,1},{1,0},{2,3},{3,2},{4,5},{5,4},{6,7},{7,6},{8,9},{9,8},{10,11... | collective-permute-start | bytes 589832 | tf_op jit(solution)/shard_map/ppermute | solution.py:405
  40.3 1.1 %collective-permute-done.7.refs_1_ = f32[24,8,256]{2,1,0:T(8,128)S(1)} collective-permute-done((f32[24,8,256]{2,1,0:T(8,128)S(1)}, f32[24,8,256]{2,1,0:T(8,128)S(1)}, u32[]{:S(2)}, u32[]{:S(2)}) %collective-permute-start.7) | collective-permute-done | bytes 196640 | tf_op jit(solution)/shard_map/ppermute | solution.py:405
  41.8 2.2 %collective-permute-start.10 = (f32[272,256]{1,0:T(8,128)S(1)}, f32[272,256]{1,0:T(8,128)S(1)}, u32[]{:S(2)}, u32[]{:S(2)}) collective-permute-start(f32[272,256]{1,0:T(8,128)S(1)} %get-tuple-element.183), channel_id=1, source_target_pairs={{0,2},{2,0},{4,6},{6,4},{8,10},{10,8},{12,14},{14,12},{1,3},{3,1},... | collective-permute-start | bytes 835592 | tf_op jit(solution)/shard_map/ppermute | solution.py:405
  45.3 1.1 %collective-permute-done.8.refs_1_ = f32[24,8,256]{2,1,0:T(8,128)S(1)} collective-permute-done((f32[24,8,256]{2,1,0:T(8,128)S(1)}, f32[24,8,256]{2,1,0:T(8,128)S(1)}, u32[]{:S(2)}, u32[]{:S(2)}) %collective-permute-start.8) | collective-permute-done | bytes 196640 | tf_op jit(solution)/shard_map/ppermute | solution.py:405
  46.3 0.9 %shard_map.166 = (f32[2,3,4,40,256]{4,3,2,1,0:T(8,128)S(1)}, f32[2,3,4,40,256]{4,3,2,1,0:T(8,128)S(1)}, f32[2,3,4,40,256]{4,3,2,1,0:T(8,128)S(1)}, f32[2,3,4,40,...) custom-call(f32[4,8,256]{2,1,0:T(8,128)S(1)} %get-tuple-element.118., ...), custom_call_target="tpu_custom_call", output_to_operand_aliasing={{0}: (2, {}), {1}: (3, {}), {2}: (4, {}), {3}: (5, {}), {6}... | custom-call | tf_op jit(solution)/shard_map/pallas_call | solution.py:390
  47.2 3.8 %collective-permute-start.9 = (f32[272,256]{1,0:T(8,128)S(1)}, f32[272,256]{1,0:T(8,128)S(1)}, u32[]{:S(2)}, u32[]{:S(2)}) collective-permute-start(f32[272,256]{1,0:T(8,128)S(1)} %get-tuple-element.181), channel_id=1, source_target_pairs={{2,4},{4,2},{6,8},{8,6},{10,12},{12,10},{14,0},{0,14},{3,5},{5,3},... | collective-permute-start | bytes 835592 | tf_op jit(solution)/shard_map/ppermute | solution.py:405
  51.0 4.5 %collective-permute-done.10.refs_1_ = f32[272,256]{1,0:T(8,128)S(1)} collective-permute-done((f32[272,256]{1,0:T(8,128)S(1)}, f32[272,256]{1,0:T(8,128)S(1)}, u32[]{:S(2)}, u32[]{:S(2)}) %collective-permute-start.10) | collective-permute-done | bytes 278560 | tf_op jit(solution)/shard_map/ppermute | solution.py:405
  56.0 1.4 %collective-permute-start.11 = (f32[24,8,256]{2,1,0:T(8,128)S(1)}, f32[24,8,256]{2,1,0:T(8,128)S(1)}, u32[]{:S(2)}, u32[]{:S(2)}) collective-permute-start(f32[24,8,256]{2,1,0:T(8,128)S(1)} %get-tuple-element.190), channel_id=1, source_target_pairs={{0,1},{1,0},{2,3},{3,2},{4,5},{5,4},{6,7},{7,6},{8,9},{9,8},{10,11... | collective-permute-start | bytes 589832 | tf_op jit(solution)/shard_map/ppermute | solution.py:405
  57.4 1.1 %collective-permute-done.11.refs_1_ = f32[24,8,256]{2,1,0:T(8,128)S(1)} collective-permute-done((f32[24,8,256]{2,1,0:T(8,128)S(1)}, f32[24,8,256]{2,1,0:T(8,128)S(1)}, u32[]{:S(2)}, u32[]{:S(2)}) %collective-permute-start.11) | collective-permute-done | bytes 196640 | tf_op jit(solution)/shard_map/ppermute | solution.py:405
  60.0 2.1 %collective-permute-start.14 = (f32[272,256]{1,0:T(8,128)S(1)}, f32[272,256]{1,0:T(8,128)S(1)}, u32[]{:S(2)}, u32[]{:S(2)}) collective-permute-start(f32[272,256]{1,0:T(8,128)S(1)} %get-tuple-element.208), channel_id=1, source_target_pairs={{0,2},{2,0},{4,6},{6,4},{8,10},{10,8},{12,14},{14,12},{1,3},{3,1},... | collective-permute-start | bytes 835592 | tf_op jit(solution)/shard_map/ppermute | solution.py:405
  63.0 3.9 %collective-permute-start.13 = (f32[272,256]{1,0:T(8,128)S(1)}, f32[272,256]{1,0:T(8,128)S(1)}, u32[]{:S(2)}, u32[]{:S(2)}) collective-permute-start(f32[272,256]{1,0:T(8,128)S(1)} %get-tuple-element.206), channel_id=1, source_target_pairs={{2,4},{4,2},{6,8},{8,6},{10,12},{12,10},{14,0},{0,14},{3,5},{5,3},... | collective-permute-start | bytes 835592 | tf_op jit(solution)/shard_map/ppermute | solution.py:405
  66.8 8.1 %collective-permute-done.14.refs_1_ = f32[272,256]{1,0:T(8,128)S(1)} collective-permute-done((f32[272,256]{1,0:T(8,128)S(1)}, f32[272,256]{1,0:T(8,128)S(1)}, u32[]{:S(2)}, u32[]{:S(2)}) %collective-permute-start.14) | collective-permute-done | bytes 278560 | tf_op jit(solution)/shard_map/ppermute | solution.py:405
  77.2 1.7 %shard_map.173 = (f32[2,3,4,32,256]{4,3,2,1,0:T(8,128)}, f32[2,3,4,32,256]{4,3,2,1,0:T(8,128)}, f32[2,3,4,32,256]{4,3,2,1,0:T(8,128)}, f32[2,3,4,32,256]{4,3,2,1,0:T(8,128)}) custom-call(f32[2,3,4,40,256]{4,3,2,1,0:T(8,128)S(1)} %get-tuple-element.220.e, f32[2,3,4,40,256]{4,3,2,1,0:T(8,128)S(1)} %get-tuple-element.221.h, ...), custom_call_target="tpu_custom_call" | custom-call | flops 4194304 | bytes 4194304 | tf_op jit(solution)/shard_map/pallas_call | solution.py:390
  (43 shorter events, 14.0 us)
Async XLA Ops:
  2.6 0.7 copy-start.4
  2.6 0.7 copy-start.5
  2.6 0.7 copy-start.6
  2.6 0.7 copy-start.1
  2.7 0.7 copy-start.2
  2.7 0.7 copy-start.3
  2.7 1.8 %collective-permute-start = (f32[52,8,256]{2,1,0:T(8,128)S(1)}, f32[52,8,256]{2,1,0:T(8,128)S(1)}, u32[]{:S(2)}, u32[]{:S(2)}) collective-permute-start(f32[52,8,256]{2,1,0:T(8,128)S(1)} %get-tuple-element.119), channel_id=1, source_target_pairs={{0,1},{1,0},{2,3},{3,2},{4,5},{5,4},{6,7},{7,6},{8,9},{9,8},{10,11... | collective-permute-start | bytes 1277960 | tf_op jit(solution)/shard_map/ppermute | solution.py:405
  5.6 16.8 %collective-permute-start.2 = (f32[312,256]{1,0:T(8,128)S(1)}, f32[312,256]{1,0:T(8,128)S(1)}, u32[]{:S(2)}, u32[]{:S(2)}) collective-permute-start(f32[312,256]{1,0:T(8,128)S(1)} %get-tuple-element.133), channel_id=1, source_target_pairs={{0,2},{2,0},{4,6},{6,4},{8,10},{10,8},{12,14},{14,12},{1,3},{3,1},... | collective-permute-start | bytes 958472 | tf_op jit(solution)/shard_map/ppermute | solution.py:405
  8.8 18.0 %collective-permute-start.1 = (f32[312,256]{1,0:T(8,128)S(1)}, f32[312,256]{1,0:T(8,128)S(1)}, u32[]{:S(2)}, u32[]{:S(2)}) collective-permute-start(f32[312,256]{1,0:T(8,128)S(1)} %get-tuple-element.131), channel_id=1, source_target_pairs={{2,4},{4,2},{6,8},{8,6},{10,12},{12,10},{14,0},{0,14},{3,5},{5,3},... | collective-permute-start | bytes 958472 | tf_op jit(solution)/shard_map/ppermute | solution.py:405
  23.0 2.0 %collective-permute-start.3 = (f32[24,8,256]{2,1,0:T(8,128)S(1)}, f32[24,8,256]{2,1,0:T(8,128)S(1)}, u32[]{:S(2)}, u32[]{:S(2)}) collective-permute-start(f32[24,8,256]{2,1,0:T(8,128)S(1)} %get-tuple-element.140), channel_id=1, source_target_pairs={{0,1},{1,0},{2,3},{3,2},{4,5},{5,4},{6,7},{7,6},{8,9},{9,8},{10,11... | collective-permute-start | bytes 589832 | tf_op jit(solution)/shard_map/ppermute | solution.py:405
  25.4 12.9 %collective-permute-start.6 = (f32[272,256]{1,0:T(8,128)S(1)}, f32[272,256]{1,0:T(8,128)S(1)}, u32[]{:S(2)}, u32[]{:S(2)}) collective-permute-start(f32[272,256]{1,0:T(8,128)S(1)} %get-tuple-element.158), channel_id=1, source_target_pairs={{0,2},{2,0},{4,6},{6,4},{8,10},{10,8},{12,14},{14,12},{1,3},{3,1},... | collective-permute-start | bytes 835592 | tf_op jit(solution)/shard_map/ppermute | solution.py:405
  27.4 1.8 %collective-permute-start.4 = (f32[24,8,256]{2,1,0:T(8,128)S(1)}, f32[24,8,256]{2,1,0:T(8,128)S(1)}, u32[]{:S(2)}, u32[]{:S(2)}) collective-permute-start(f32[24,8,256]{2,1,0:T(8,128)S(1)} %get-tuple-element.150), channel_id=1, source_target_pairs={{0,1},{1,0},{2,3},{3,2},{4,5},{5,4},{6,7},{7,6},{8,9},{9,8},{10,11... | collective-permute-start | bytes 589832 | tf_op jit(solution)/shard_map/ppermute | solution.py:405
  30.1 13.9 %collective-permute-start.5 = (f32[272,256]{1,0:T(8,128)S(1)}, f32[272,256]{1,0:T(8,128)S(1)}, u32[]{:S(2)}, u32[]{:S(2)}) collective-permute-start(f32[272,256]{1,0:T(8,128)S(1)} %get-tuple-element.156), channel_id=1, source_target_pairs={{2,4},{4,2},{6,8},{8,6},{10,12},{12,10},{14,0},{0,14},{3,5},{5,3},... | collective-permute-start | bytes 835592 | tf_op jit(solution)/shard_map/ppermute | solution.py:405
  38.9 2.5 %collective-permute-start.7 = (f32[24,8,256]{2,1,0:T(8,128)S(1)}, f32[24,8,256]{2,1,0:T(8,128)S(1)}, u32[]{:S(2)}, u32[]{:S(2)}) collective-permute-start(f32[24,8,256]{2,1,0:T(8,128)S(1)} %get-tuple-element.165), channel_id=1, source_target_pairs={{0,1},{1,0},{2,3},{3,2},{4,5},{5,4},{6,7},{7,6},{8,9},{9,8},{10,11... | collective-permute-start | bytes 589832 | tf_op jit(solution)/shard_map/ppermute | solution.py:405
  41.8 13.7 %collective-permute-start.10 = (f32[272,256]{1,0:T(8,128)S(1)}, f32[272,256]{1,0:T(8,128)S(1)}, u32[]{:S(2)}, u32[]{:S(2)}) collective-permute-start(f32[272,256]{1,0:T(8,128)S(1)} %get-tuple-element.183), channel_id=1, source_target_pairs={{0,2},{2,0},{4,6},{6,4},{8,10},{10,8},{12,14},{14,12},{1,3},{3,1},... | collective-permute-start | bytes 835592 | tf_op jit(solution)/shard_map/ppermute | solution.py:405
  44.5 1.8 %collective-permute-start.8 = (f32[24,8,256]{2,1,0:T(8,128)S(1)}, f32[24,8,256]{2,1,0:T(8,128)S(1)}, u32[]{:S(2)}, u32[]{:S(2)}) collective-permute-start(f32[24,8,256]{2,1,0:T(8,128)S(1)} %get-tuple-element.175), channel_id=1, source_target_pairs={{0,1},{1,0},{2,3},{3,2},{4,5},{5,4},{6,7},{7,6},{8,9},{9,8},{10,11... | collective-permute-start | bytes 589832 | tf_op jit(solution)/shard_map/ppermute | solution.py:405
  47.2 11.7 %collective-permute-start.9 = (f32[272,256]{1,0:T(8,128)S(1)}, f32[272,256]{1,0:T(8,128)S(1)}, u32[]{:S(2)}, u32[]{:S(2)}) collective-permute-start(f32[272,256]{1,0:T(8,128)S(1)} %get-tuple-element.181), channel_id=1, source_target_pairs={{2,4},{4,2},{6,8},{8,6},{10,12},{12,10},{14,0},{0,14},{3,5},{5,3},... | collective-permute-start | bytes 835592 | tf_op jit(solution)/shard_map/ppermute | solution.py:405
  56.0 2.5 %collective-permute-start.11 = (f32[24,8,256]{2,1,0:T(8,128)S(1)}, f32[24,8,256]{2,1,0:T(8,128)S(1)}, u32[]{:S(2)}, u32[]{:S(2)}) collective-permute-start(f32[24,8,256]{2,1,0:T(8,128)S(1)} %get-tuple-element.190), channel_id=1, source_target_pairs={{0,1},{1,0},{2,3},{3,2},{4,5},{5,4},{6,7},{7,6},{8,9},{9,8},{10,11... | collective-permute-start | bytes 589832 | tf_op jit(solution)/shard_map/ppermute | solution.py:405
  59.5 2.5 %collective-permute-start.12 = (f32[24,8,256]{2,1,0:T(8,128)S(1)}, f32[24,8,256]{2,1,0:T(8,128)S(1)}, u32[]{:S(2)}, u32[]{:S(2)}) collective-permute-start(f32[24,8,256]{2,1,0:T(8,128)S(1)} %get-tuple-element.200), channel_id=1, source_target_pairs={{0,1},{1,0},{2,3},{3,2},{4,5},{5,4},{6,7},{7,6},{8,9},{9,8},{10,11... | collective-permute-start | bytes 589832 | tf_op jit(solution)/shard_map/ppermute | solution.py:405
  60.0 15.0 %collective-permute-start.14 = (f32[272,256]{1,0:T(8,128)S(1)}, f32[272,256]{1,0:T(8,128)S(1)}, u32[]{:S(2)}, u32[]{:S(2)}) collective-permute-start(f32[272,256]{1,0:T(8,128)S(1)} %get-tuple-element.208), channel_id=1, source_target_pairs={{0,2},{2,0},{4,6},{6,4},{8,10},{10,8},{12,14},{14,12},{1,3},{3,1},... | collective-permute-start | bytes 835592 | tf_op jit(solution)/shard_map/ppermute | solution.py:405
  63.0 12.5 %collective-permute-start.13 = (f32[272,256]{1,0:T(8,128)S(1)}, f32[272,256]{1,0:T(8,128)S(1)}, u32[]{:S(2)}, u32[]{:S(2)}) collective-permute-start(f32[272,256]{1,0:T(8,128)S(1)} %get-tuple-element.206), channel_id=1, source_target_pairs={{2,4},{4,2},{6,8},{8,6},{10,12},{12,10},{14,0},{0,14},{3,5},{5,3},... | collective-permute-start | bytes 835592 | tf_op jit(solution)/shard_map/ppermute | solution.py:405
  75.5 0.7 copy-start
  76.5 2.4 %collective-permute-start.15 = (f32[2,4,8,128]{3,2,1,0:T(8,128)S(1)}, f32[2,4,8,128]{3,2,1,0:T(8,128)S(1)}, u32[]{:S(2)}, u32[]{:S(2)}) collective-permute-start(f32[2,4,8,128]{3,2,1,0:T(8,128)S(1)} %shard_map.174.own), channel_id=1, source_target_pairs={{0,1},{1,0},{2,3},{3,2},{4,5},{5,4},{6,7},{7,6},{8,9},{9,8},{10,11... | collective-permute-start | bytes 98312 | tf_op jit(solution)/shard_map/ppermute | solution.py:405

commit v3 on v2

--- a/solution.py
+++ b/solution.py
@@ -462,6 +462,7 @@
                 keep + [e0_shape, ((size + rows + EDGE, depth), f32), rec_shape],
                 {0: 0, 1: 1, 2: 2, 3: 3, 5: 6},
             )
+            out, msg[ORDER[0]] = lax.optimization_barrier((out, msg[ORDER[0]]))
         msg[which] = far[which] = swap(out, "gx", which)
     for step in range(0, STEPS, 2):
         final = step == STEPS - 2

time: 79.8 us -> 77.5 us (0.971)
  starting transfers between devices: 29.4 us -> 28 us
  waiting for transfers between devices: 32.9 us -> 31.9 us
    ppermute x16, starting transfers between devices: 29.4 us -> 28 us  [swap(): lax.ppermute(block, axis, [q for a, b in pairs for q in ((a, b), (b, a))])]
    ppermute x16, waiting for transfers between devices: 32.9 us -> 31.9 us  [swap(): lax.ppermute(block, axis, [q for a, b in pairs for q in ((a, b), (b, a))])]
  transfers between devices with their start and end apart: 16 -> 16, of which waited for: 10 -> 12; matrix products, arithmetic and copies ran while one was open for 0% -> 0% of each run, Pallas kernels for 13% -> 14%
where the time goes in v3:
time: 77.5 us; the launch traced here: 77.2 us
  waiting for transfers between devices  31.9 us (41%)
  starting transfers between devices  28 us (36%)
  Pallas kernels  15.8 us (20%)
  between operations  0.85 us (1%)
    ppermute x16, waiting for transfers between devices, swap(): lax.ppermute(block, axis, [q for a, b in pairs for q in ((a, b), (b, a))])  31.9 us
    ppermute x16, starting transfers between devices, swap(): lax.ppermute(block, axis, [q for a, b in pairs for q in ((a, b), (b, a))])  28 us
    pallas_call x21, Pallas kernels, call(): pl.pallas_call(body, out_shape=shapes, in_specs=[sm if i in smem else hbm...  15.8 us
  transfers between devices with their start and end apart: 16, of which 12 were waited for; matrix products, arithmetic and copies ran while one was open for 0% of the time, Pallas kernels for 14%

profile of v3, /device:TPU:1, one launch (start us, length us, event | category | flops | bytes accessed | tf_op | source)
XLA Modules:
  0.0 77.2 jit_solution(3754878847284741480)
XLA Ops:
  0.6 2.0 %shard_map.155 = (f32[2,3,4,40,256]{4,3,2,1,0:T(8,128)S(1)}, f32[2,3,4,40,256]{4,3,2,1,0:T(8,128)S(1)}, f32[2,3,4,40,256]{4,3,2,1,0:T(8,128)S(1)}, f32[2,3,4,40,...) custom-call(f32[2,3,4,32,256]{4,3,2,1,0:T(8,128)} %e_in.1, f32[2,3,4,32,256]{4,3,2,1,0:T(8,128)} %h_in.1, ...), custom_call_target="tpu_custom_call" | custom-call | tf_op jit(solution)/shard_map/pallas_call | solution.py:390
  4.5 1.1 %shard_map.157 = (f32[2,3,4,40,256]{4,3,2,1,0:T(8,128)S(1)}, f32[2,3,4,40,256]{4,3,2,1,0:T(8,128)S(1)}, f32[2,3,4,40,256]{4,3,2,1,0:T(8,128)S(1)}, f32[2,3,4,40,...) custom-call(f32[4,8,256]{2,1,0:T(8,128)S(1)} %get-tuple-element.120., ...), custom_call_target="tpu_custom_call", output_to_operand_aliasing={{0}: (7, {}), {1}: (8, {}), {2}: (9, {}), {3}: (10, {}), {4... | custom-call | tf_op jit(solution)/shard_map/pallas_call | solution.py:390
  5.6 2.3 %collective-permute-start.1 = (f32[312,256]{1,0:T(8,128)S(1)}, f32[312,256]{1,0:T(8,128)S(1)}, u32[]{:S(2)}, u32[]{:S(2)}) collective-permute-start(f32[312,256]{1,0:T(8,128)S(1)} %get-tuple-element.134), channel_id=1, source_target_pairs={{0,2},{2,0},{4,6},{6,4},{8,10},{10,8},{12,14},{14,12},{1,3},{3,1},... | collective-permute-start | bytes 958472 | tf_op jit(solution)/shard_map/ppermute | solution.py:405
  8.8 6.8 %collective-permute-done.1.refs_1_.refs_3_ = f32[312,256]{1,0:T(8,128)S(1)} collective-permute-done((f32[312,256]{1,0:T(8,128)S(1)}, f32[312,256]{1,0:T(8,128)S(1)}, u32[]{:S(2)}, u32[]{:S(2)}) %collective-permute-start.1) | collective-permute-done | bytes 319520 | tf_op jit(solution)/shard_map/ppermute | solution.py:405
  15.6 4.2 %collective-permute-start.2 = (f32[312,256]{1,0:T(8,128)S(1)}, f32[312,256]{1,0:T(8,128)S(1)}, u32[]{:S(2)}, u32[]{:S(2)}) collective-permute-start(f32[312,256]{1,0:T(8,128)S(1)} %get-tuple-element.135), channel_id=1, source_target_pairs={{2,4},{4,2},{6,8},{8,6},{10,12},{12,10},{14,0},{0,14},{3,5},{5,3},... | collective-permute-start | bytes 958472 | tf_op jit(solution)/shard_map/ppermute | solution.py:405
  20.3 1.5 %collective-permute-start.3 = (f32[24,8,256]{2,1,0:T(8,128)S(1)}, f32[24,8,256]{2,1,0:T(8,128)S(1)}, u32[]{:S(2)}, u32[]{:S(2)}) collective-permute-start(f32[24,8,256]{2,1,0:T(8,128)S(1)} %get-tuple-element.144), channel_id=1, source_target_pairs={{0,1},{1,0},{2,3},{3,2},{4,5},{5,4},{6,7},{7,6},{8,9},{9,8},{10,11... | collective-permute-start | bytes 589832 | tf_op jit(solution)/shard_map/ppermute | solution.py:405
  21.9 1.1 %collective-permute-done.3.refs_1_ = f32[24,8,256]{2,1,0:T(8,128)S(1)} collective-permute-done((f32[24,8,256]{2,1,0:T(8,128)S(1)}, f32[24,8,256]{2,1,0:T(8,128)S(1)}, u32[]{:S(2)}, u32[]{:S(2)}) %collective-permute-start.3) | collective-permute-done | bytes 196640 | tf_op jit(solution)/shard_map/ppermute | solution.py:405
  23.4 3.0 %collective-permute-done.2.refs_1_.refs_3_ = f32[312,256]{1,0:T(8,128)S(1)} collective-permute-done((f32[312,256]{1,0:T(8,128)S(1)}, f32[312,256]{1,0:T(8,128)S(1)}, u32[]{:S(2)}, u32[]{:S(2)}) %collective-permute-start.2) | collective-permute-done | bytes 319520 | tf_op jit(solution)/shard_map/ppermute | solution.py:405
  27.0 2.0 %collective-permute-start.4 = (f32[24,8,256]{2,1,0:T(8,128)S(1)}, f32[24,8,256]{2,1,0:T(8,128)S(1)}, u32[]{:S(2)}, u32[]{:S(2)}) collective-permute-start(f32[24,8,256]{2,1,0:T(8,128)S(1)} %get-tuple-element.154), channel_id=1, source_target_pairs={{0,1},{1,0},{2,3},{3,2},{4,5},{5,4},{6,7},{7,6},{8,9},{9,8},{10,11... | collective-permute-start | bytes 589832 | tf_op jit(solution)/shard_map/ppermute | solution.py:405
  29.0 1.1 %collective-permute-done.4.refs_1_ = f32[24,8,256]{2,1,0:T(8,128)S(1)} collective-permute-done((f32[24,8,256]{2,1,0:T(8,128)S(1)}, f32[24,8,256]{2,1,0:T(8,128)S(1)}, u32[]{:S(2)}, u32[]{:S(2)}) %collective-permute-start.4) | collective-permute-done | bytes 196640 | tf_op jit(solution)/shard_map/ppermute | solution.py:405
  30.1 0.9 %shard_map.162 = (f32[2,3,4,40,256]{4,3,2,1,0:T(8,128)S(1)}, f32[2,3,4,40,256]{4,3,2,1,0:T(8,128)S(1)}, f32[2,3,4,40,256]{4,3,2,1,0:T(8,128)S(1)}, f32[2,3,4,40,...) custom-call(f32[4,8,256]{2,1,0:T(8,128)S(1)} %get-tuple-element.120., ...), custom_call_target="tpu_custom_call", output_to_operand_aliasing={{0}: (2, {}), {1}: (3, {}), {2}: (4, {}), {3}: (5, {}), {6}... | custom-call | tf_op jit(solution)/shard_map/pallas_call | solution.py:390
  30.9 4.3 %collective-permute-start.5 = (f32[272,256]{1,0:T(8,128)S(1)}, f32[272,256]{1,0:T(8,128)S(1)}, u32[]{:S(2)}, u32[]{:S(2)}) collective-permute-start(f32[272,256]{1,0:T(8,128)S(1)} %get-tuple-element.160), channel_id=1, source_target_pairs={{2,4},{4,2},{6,8},{8,6},{10,12},{12,10},{14,0},{0,14},{3,5},{5,3},... | collective-permute-start | bytes 835592 | tf_op jit(solution)/shard_map/ppermute | solution.py:405
  36.6 1.1 %collective-permute-done.7.refs_1_ = f32[24,8,256]{2,1,0:T(8,128)S(1)} collective-permute-done((f32[24,8,256]{2,1,0:T(8,128)S(1)}, f32[24,8,256]{2,1,0:T(8,128)S(1)}, u32[]{:S(2)}, u32[]{:S(2)}) %collective-permute-start.7) | collective-permute-done | bytes 196640 | tf_op jit(solution)/shard_map/ppermute | solution.py:405
  38.1 3.7 %collective-permute-done.5.refs_1_ = f32[272,256]{1,0:T(8,128)S(1)} collective-permute-done((f32[272,256]{1,0:T(8,128)S(1)}, f32[272,256]{1,0:T(8,128)S(1)}, u32[]{:S(2)}, u32[]{:S(2)}) %collective-permute-start.5) | collective-permute-done | bytes 278560 | tf_op jit(solution)/shard_map/ppermute | solution.py:405
  42.4 1.2 %collective-permute-start.8 = (f32[24,8,256]{2,1,0:T(8,128)S(1)}, f32[24,8,256]{2,1,0:T(8,128)S(1)}, u32[]{:S(2)}, u32[]{:S(2)}) collective-permute-start(f32[24,8,256]{2,1,0:T(8,128)S(1)} %get-tuple-element.179), channel_id=1, source_target_pairs={{0,1},{1,0},{2,3},{3,2},{4,5},{5,4},{6,7},{7,6},{8,9},{9,8},{10,11... | collective-permute-start | bytes 589832 | tf_op jit(solution)/shard_map/ppermute | solution.py:405
  43.6 1.1 %collective-permute-done.8.refs_1_ = f32[24,8,256]{2,1,0:T(8,128)S(1)} collective-permute-done((f32[24,8,256]{2,1,0:T(8,128)S(1)}, f32[24,8,256]{2,1,0:T(8,128)S(1)}, u32[]{:S(2)}, u32[]{:S(2)}) %collective-permute-start.8) | collective-permute-done | bytes 196640 | tf_op jit(solution)/shard_map/ppermute | solution.py:405
  45.6 4.3 %collective-permute-start.9 = (f32[272,256]{1,0:T(8,128)S(1)}, f32[272,256]{1,0:T(8,128)S(1)}, u32[]{:S(2)}, u32[]{:S(2)}) collective-permute-start(f32[272,256]{1,0:T(8,128)S(1)} %get-tuple-element.185), channel_id=1, source_target_pairs={{2,4},{4,2},{6,8},{8,6},{10,12},{12,10},{14,0},{0,14},{3,5},{5,3},... | collective-permute-start | bytes 835592 | tf_op jit(solution)/shard_map/ppermute | solution.py:405
  51.2 1.1 %collective-permute-done.11.refs_1_ = f32[24,8,256]{2,1,0:T(8,128)S(1)} collective-permute-done((f32[24,8,256]{2,1,0:T(8,128)S(1)}, f32[24,8,256]{2,1,0:T(8,128)S(1)}, u32[]{:S(2)}, u32[]{:S(2)}) %collective-permute-start.11) | collective-permute-done | bytes 196640 | tf_op jit(solution)/shard_map/ppermute | solution.py:405
  52.7 3.8 %collective-permute-done.9.refs_1_ = f32[272,256]{1,0:T(8,128)S(1)} collective-permute-done((f32[272,256]{1,0:T(8,128)S(1)}, f32[272,256]{1,0:T(8,128)S(1)}, u32[]{:S(2)}, u32[]{:S(2)}) %collective-permute-start.9) | collective-permute-done | bytes 278560 | tf_op jit(solution)/shard_map/ppermute | solution.py:405
  57.0 1.1 %collective-permute-start.12 = (f32[24,8,256]{2,1,0:T(8,128)S(1)}, f32[24,8,256]{2,1,0:T(8,128)S(1)}, u32[]{:S(2)}, u32[]{:S(2)}) collective-permute-start(f32[24,8,256]{2,1,0:T(8,128)S(1)} %get-tuple-element.204), channel_id=1, source_target_pairs={{0,1},{1,0},{2,3},{3,2},{4,5},{5,4},{6,7},{7,6},{8,9},{9,8},{10,11... | collective-permute-start | bytes 589832 | tf_op jit(solution)/shard_map/ppermute | solution.py:405
  58.2 1.1 %collective-permute-done.12.refs_1_ = f32[24,8,256]{2,1,0:T(8,128)S(1)} collective-permute-done((f32[24,8,256]{2,1,0:T(8,128)S(1)}, f32[24,8,256]{2,1,0:T(8,128)S(1)}, u32[]{:S(2)}, u32[]{:S(2)}) %collective-permute-start.12) | collective-permute-done | bytes 196640 | tf_op jit(solution)/shard_map/ppermute | solution.py:405
  60.1 4.3 %collective-permute-start.13 = (f32[272,256]{1,0:T(8,128)S(1)}, f32[272,256]{1,0:T(8,128)S(1)}, u32[]{:S(2)}, u32[]{:S(2)}) collective-permute-start(f32[272,256]{1,0:T(8,128)S(1)} %get-tuple-element.210), channel_id=1, source_target_pairs={{2,4},{4,2},{6,8},{8,6},{10,12},{12,10},{14,0},{0,14},{3,5},{5,3},... | collective-permute-start | bytes 835592 | tf_op jit(solution)/shard_map/ppermute | solution.py:405
  64.5 7.9 %collective-permute-done.14.refs_1_ = f32[272,256]{1,0:T(8,128)S(1)} collective-permute-done((f32[272,256]{1,0:T(8,128)S(1)}, f32[272,256]{1,0:T(8,128)S(1)}, u32[]{:S(2)}, u32[]{:S(2)}) %collective-permute-start.14) | collective-permute-done | bytes 278560 | tf_op jit(solution)/shard_map/ppermute | solution.py:405
  74.8 1.7 %shard_map.173 = (f32[2,3,4,32,256]{4,3,2,1,0:T(8,128)}, f32[2,3,4,32,256]{4,3,2,1,0:T(8,128)}, f32[2,3,4,32,256]{4,3,2,1,0:T(8,128)}, f32[2,3,4,32,256]{4,3,2,1,0:T(8,128)}) custom-call(f32[2,3,4,40,256]{4,3,2,1,0:T(8,128)S(1)} %get-tuple-element.224.e, f32[2,3,4,40,256]{4,3,2,1,0:T(8,128)S(1)} %get-tuple-element.225.h, ...), custom_call_target="tpu_custom_call" | custom-call | flops 4194304 | bytes 4194304 | tf_op jit(solution)/shard_map/pallas_call | solution.py:390
  (43 shorter events, 13.8 us)
Async XLA Ops:
  2.6 0.7 copy-start.4
  2.6 0.7 copy-start.5
  2.6 0.7 copy-start.6
  2.6 0.7 copy-start.1
  2.7 0.7 copy-start.2
  2.7 0.7 copy-start.3
  2.7 1.8 %collective-permute-start = (f32[52,8,256]{2,1,0:T(8,128)S(1)}, f32[52,8,256]{2,1,0:T(8,128)S(1)}, u32[]{:S(2)}, u32[]{:S(2)}) collective-permute-start(f32[52,8,256]{2,1,0:T(8,128)S(1)} %get-tuple-element.121), channel_id=1, source_target_pairs={{0,1},{1,0},{2,3},{3,2},{4,5},{5,4},{6,7},{7,6},{8,9},{9,8},{10,11... | collective-permute-start | bytes 1277960 | tf_op jit(solution)/shard_map/ppermute | solution.py:405
  5.6 9.9 %collective-permute-start.1 = (f32[312,256]{1,0:T(8,128)S(1)}, f32[312,256]{1,0:T(8,128)S(1)}, u32[]{:S(2)}, u32[]{:S(2)}) collective-permute-start(f32[312,256]{1,0:T(8,128)S(1)} %get-tuple-element.134), channel_id=1, source_target_pairs={{0,2},{2,0},{4,6},{6,4},{8,10},{10,8},{12,14},{14,12},{1,3},{3,1},... | collective-permute-start | bytes 958472 | tf_op jit(solution)/shard_map/ppermute | solution.py:405
  15.6 10.8 %collective-permute-start.2 = (f32[312,256]{1,0:T(8,128)S(1)}, f32[312,256]{1,0:T(8,128)S(1)}, u32[]{:S(2)}, u32[]{:S(2)}) collective-permute-start(f32[312,256]{1,0:T(8,128)S(1)} %get-tuple-element.135), channel_id=1, source_target_pairs={{2,4},{4,2},{6,8},{8,6},{10,12},{12,10},{14,0},{0,14},{3,5},{5,3},... | collective-permute-start | bytes 958472 | tf_op jit(solution)/shard_map/ppermute | solution.py:405
  20.3 2.6 %collective-permute-start.3 = (f32[24,8,256]{2,1,0:T(8,128)S(1)}, f32[24,8,256]{2,1,0:T(8,128)S(1)}, u32[]{:S(2)}, u32[]{:S(2)}) collective-permute-start(f32[24,8,256]{2,1,0:T(8,128)S(1)} %get-tuple-element.144), channel_id=1, source_target_pairs={{0,1},{1,0},{2,3},{3,2},{4,5},{5,4},{6,7},{7,6},{8,9},{9,8},{10,11... | collective-permute-start | bytes 589832 | tf_op jit(solution)/shard_map/ppermute | solution.py:405
  23.3 11.9 %collective-permute-start.6 = (f32[272,256]{1,0:T(8,128)S(1)}, f32[272,256]{1,0:T(8,128)S(1)}, u32[]{:S(2)}, u32[]{:S(2)}) collective-permute-start(f32[272,256]{1,0:T(8,128)S(1)} %get-tuple-element.162), channel_id=1, source_target_pairs={{0,2},{2,0},{4,6},{6,4},{8,10},{10,8},{12,14},{14,12},{1,3},{3,1},... | collective-permute-start | bytes 835592 | tf_op jit(solution)/shard_map/ppermute | solution.py:405
  27.0 3.1 %collective-permute-start.4 = (f32[24,8,256]{2,1,0:T(8,128)S(1)}, f32[24,8,256]{2,1,0:T(8,128)S(1)}, u32[]{:S(2)}, u32[]{:S(2)}) collective-permute-start(f32[24,8,256]{2,1,0:T(8,128)S(1)} %get-tuple-element.154), channel_id=1, source_target_pairs={{0,1},{1,0},{2,3},{3,2},{4,5},{5,4},{6,7},{7,6},{8,9},{9,8},{10,11... | collective-permute-start | bytes 589832 | tf_op jit(solution)/shard_map/ppermute | solution.py:405
  30.9 10.9 %collective-permute-start.5 = (f32[272,256]{1,0:T(8,128)S(1)}, f32[272,256]{1,0:T(8,128)S(1)}, u32[]{:S(2)}, u32[]{:S(2)}) collective-permute-start(f32[272,256]{1,0:T(8,128)S(1)} %get-tuple-element.160), channel_id=1, source_target_pairs={{2,4},{4,2},{6,8},{8,6},{10,12},{12,10},{14,0},{0,14},{3,5},{5,3},... | collective-permute-start | bytes 835592 | tf_op jit(solution)/shard_map/ppermute | solution.py:405
  35.9 1.8 %collective-permute-start.7 = (f32[24,8,256]{2,1,0:T(8,128)S(1)}, f32[24,8,256]{2,1,0:T(8,128)S(1)}, u32[]{:S(2)}, u32[]{:S(2)}) collective-permute-start(f32[24,8,256]{2,1,0:T(8,128)S(1)} %get-tuple-element.169), channel_id=1, source_target_pairs={{0,1},{1,0},{2,3},{3,2},{4,5},{5,4},{6,7},{7,6},{8,9},{9,8},{10,11... | collective-permute-start | bytes 589832 | tf_op jit(solution)/shard_map/ppermute | solution.py:405
  38.1 11.9 %collective-permute-start.10 = (f32[272,256]{1,0:T(8,128)S(1)}, f32[272,256]{1,0:T(8,128)S(1)}, u32[]{:S(2)}, u32[]{:S(2)}) collective-permute-start(f32[272,256]{1,0:T(8,128)S(1)} %get-tuple-element.187), channel_id=1, source_target_pairs={{0,2},{2,0},{4,6},{6,4},{8,10},{10,8},{12,14},{14,12},{1,3},{3,1},... | collective-permute-start | bytes 835592 | tf_op jit(solution)/shard_map/ppermute | solution.py:405
  42.4 2.3 %collective-permute-start.8 = (f32[24,8,256]{2,1,0:T(8,128)S(1)}, f32[24,8,256]{2,1,0:T(8,128)S(1)}, u32[]{:S(2)}, u32[]{:S(2)}) collective-permute-start(f32[24,8,256]{2,1,0:T(8,128)S(1)} %get-tuple-element.179), channel_id=1, source_target_pairs={{0,1},{1,0},{2,3},{3,2},{4,5},{5,4},{6,7},{7,6},{8,9},{9,8},{10,11... | collective-permute-start | bytes 589832 | tf_op jit(solution)/shard_map/ppermute | solution.py:405
  45.6 10.9 %collective-permute-start.9 = (f32[272,256]{1,0:T(8,128)S(1)}, f32[272,256]{1,0:T(8,128)S(1)}, u32[]{:S(2)}, u32[]{:S(2)}) collective-permute-start(f32[272,256]{1,0:T(8,128)S(1)} %get-tuple-element.185), channel_id=1, source_target_pairs={{2,4},{4,2},{6,8},{8,6},{10,12},{12,10},{14,0},{0,14},{3,5},{5,3},... | collective-permute-start | bytes 835592 | tf_op jit(solution)/shard_map/ppermute | solution.py:405
  50.5 1.8 %collective-permute-start.11 = (f32[24,8,256]{2,1,0:T(8,128)S(1)}, f32[24,8,256]{2,1,0:T(8,128)S(1)}, u32[]{:S(2)}, u32[]{:S(2)}) collective-permute-start(f32[24,8,256]{2,1,0:T(8,128)S(1)} %get-tuple-element.194), channel_id=1, source_target_pairs={{0,1},{1,0},{2,3},{3,2},{4,5},{5,4},{6,7},{7,6},{8,9},{9,8},{10,11... | collective-permute-start | bytes 589832 | tf_op jit(solution)/shard_map/ppermute | solution.py:405
  57.0 2.2 %collective-permute-start.12 = (f32[24,8,256]{2,1,0:T(8,128)S(1)}, f32[24,8,256]{2,1,0:T(8,128)S(1)}, u32[]{:S(2)}, u32[]{:S(2)}) collective-permute-start(f32[24,8,256]{2,1,0:T(8,128)S(1)} %get-tuple-element.204), channel_id=1, source_target_pairs={{0,1},{1,0},{2,3},{3,2},{4,5},{5,4},{6,7},{7,6},{8,9},{9,8},{10,11... | collective-permute-start | bytes 589832 | tf_op jit(solution)/shard_map/ppermute | solution.py:405
  58.2 14.2 %collective-permute-start.14 = (f32[272,256]{1,0:T(8,128)S(1)}, f32[272,256]{1,0:T(8,128)S(1)}, u32[]{:S(2)}, u32[]{:S(2)}) collective-permute-start(f32[272,256]{1,0:T(8,128)S(1)} %get-tuple-element.212), channel_id=1, source_target_pairs={{0,2},{2,0},{4,6},{6,4},{8,10},{10,8},{12,14},{14,12},{1,3},{3,1},... | collective-permute-start | bytes 835592 | tf_op jit(solution)/shard_map/ppermute | solution.py:405
  60.1 12.8 %collective-permute-start.13 = (f32[272,256]{1,0:T(8,128)S(1)}, f32[272,256]{1,0:T(8,128)S(1)}, u32[]{:S(2)}, u32[]{:S(2)}) collective-permute-start(f32[272,256]{1,0:T(8,128)S(1)} %get-tuple-element.210), channel_id=1, source_target_pairs={{2,4},{4,2},{6,8},{8,6},{10,12},{12,10},{14,0},{0,14},{3,5},{5,3},... | collective-permute-start | bytes 835592 | tf_op jit(solution)/shard_map/ppermute | solution.py:405
  73.0 0.7 copy-start
  73.9 2.6 %collective-permute-start.15 = (f32[2,4,8,128]{3,2,1,0:T(8,128)S(1)}, f32[2,4,8,128]{3,2,1,0:T(8,128)S(1)}, u32[]{:S(2)}, u32[]{:S(2)}) collective-permute-start(f32[2,4,8,128]{3,2,1,0:T(8,128)S(1)} %shard_map.174.own), channel_id=1, source_target_pairs={{0,1},{1,0},{2,3},{3,2},{4,5},{5,4},{6,7},{7,6},{8,9},{9,8},{10,11... | collective-permute-start | bytes 98312 | tf_op jit(solution)/shard_map/ppermute | solution.py:405

commit v4 on v3

--- a/solution.py
+++ b/solution.py
@@ -280,7 +280,7 @@
             out[2 * half + 16 :] = coef[0, 0]
 
     by_side(which, upper, lower)
-    if second:
+    if second and step < STEPS - 2:
         inner_part(rows, step, (e, h, p, j, rec), coef)
 
 
@@ -489,6 +489,13 @@
                 rec, out = out, e0[which]
                 e0[which] = state.pop()
             msg[which] = swap(out, "gx", which)
+            if second and step == STEPS - 4:
+                *state, rec = call(
+                    lambda *refs: inner_part(rows, STEPS - 2, refs[6:], refs[5]),
+                    (*state, rec, coef),
+                    keep + [rec_shape],
+                    {i: i for i in range(5)},
+                )
     e, h, p, j = state
     (harm,) = call(harmonics_body, (rec, waves), [((2, planes, HARM, 128), f32)])
     other = swap(harm, "gy", 0)

time: 77.5 us -> 77.5 us (level)
    pallas_call x21 -> x22, Pallas kernels: 15.8 us -> 15.8 us  [call(): pl.pallas_call(body, out_shape=shapes, in_specs=[sm if i in smem else hbm...]
where the time goes in v4:
time: 77.5 us; the launch traced here: 77.2 us
  waiting for transfers between devices  31.9 us (41%)
  starting transfers between devices  28 us (36%)
  Pallas kernels  15.8 us (20%)
  between operations  0.86 us (1%)
    ppermute x16, waiting for transfers between devices, swap(): lax.ppermute(block, axis, [q for a, b in pairs for q in ((a, b), (b, a))])  31.9 us
    ppermute x16, starting transfers between devices, swap(): lax.ppermute(block, axis, [q for a, b in pairs for q in ((a, b), (b, a))])  28 us
    pallas_call x22, Pallas kernels, call(): pl.pallas_call(body, out_shape=shapes, in_specs=[sm if i in smem else hbm...  15.8 us
  transfers between devices with their start and end apart: 16, of which 12 were waited for; matrix products, arithmetic and copies ran while one was open for 0% of the time, Pallas kernels for 14%

profile of v4, /device:TPU:1, one launch (start us, length us, event | category | flops | bytes accessed | tf_op | source)
XLA Modules:
  0.0 77.2 jit_solution(485613398584217362)
XLA Ops:
  0.6 2.0 %shard_map.155 = (f32[2,3,4,40,256]{4,3,2,1,0:T(8,128)S(1)}, f32[2,3,4,40,256]{4,3,2,1,0:T(8,128)S(1)}, f32[2,3,4,40,256]{4,3,2,1,0:T(8,128)S(1)}, f32[2,3,4,40,...) custom-call(f32[2,3,4,32,256]{4,3,2,1,0:T(8,128)} %e_in.1, f32[2,3,4,32,256]{4,3,2,1,0:T(8,128)} %h_in.1, ...), custom_call_target="tpu_custom_call" | custom-call | tf_op jit(solution)/shard_map/pallas_call | solution.py:390
  4.5 1.1 %shard_map.157 = (f32[2,3,4,40,256]{4,3,2,1,0:T(8,128)S(1)}, f32[2,3,4,40,256]{4,3,2,1,0:T(8,128)S(1)}, f32[2,3,4,40,256]{4,3,2,1,0:T(8,128)S(1)}, f32[2,3,4,40,...) custom-call(f32[4,8,256]{2,1,0:T(8,128)S(1)} %get-tuple-element.125., ...), custom_call_target="tpu_custom_call", output_to_operand_aliasing={{0}: (7, {}), {1}: (8, {}), {2}: (9, {}), {3}: (10, {}), {4... | custom-call | tf_op jit(solution)/shard_map/pallas_call | solution.py:390
  5.6 2.3 %collective-permute-start.1 = (f32[312,256]{1,0:T(8,128)S(1)}, f32[312,256]{1,0:T(8,128)S(1)}, u32[]{:S(2)}, u32[]{:S(2)}) collective-permute-start(f32[312,256]{1,0:T(8,128)S(1)} %get-tuple-element.139), channel_id=1, source_target_pairs={{0,2},{2,0},{4,6},{6,4},{8,10},{10,8},{12,14},{14,12},{1,3},{3,1},... | collective-permute-start | bytes 958472 | tf_op jit(solution)/shard_map/ppermute | solution.py:405
  8.8 6.8 %collective-permute-done.1.refs_1_.refs_3_ = f32[312,256]{1,0:T(8,128)S(1)} collective-permute-done((f32[312,256]{1,0:T(8,128)S(1)}, f32[312,256]{1,0:T(8,128)S(1)}, u32[]{:S(2)}, u32[]{:S(2)}) %collective-permute-start.1) | collective-permute-done | bytes 319520 | tf_op jit(solution)/shard_map/ppermute | solution.py:405
  15.6 4.2 %collective-permute-start.2 = (f32[312,256]{1,0:T(8,128)S(1)}, f32[312,256]{1,0:T(8,128)S(1)}, u32[]{:S(2)}, u32[]{:S(2)}) collective-permute-start(f32[312,256]{1,0:T(8,128)S(1)} %get-tuple-element.140), channel_id=1, source_target_pairs={{2,4},{4,2},{6,8},{8,6},{10,12},{12,10},{14,0},{0,14},{3,5},{5,3},... | collective-permute-start | bytes 958472 | tf_op jit(solution)/shard_map/ppermute | solution.py:405
  20.3 1.5 %collective-permute-start.3 = (f32[24,8,256]{2,1,0:T(8,128)S(1)}, f32[24,8,256]{2,1,0:T(8,128)S(1)}, u32[]{:S(2)}, u32[]{:S(2)}) collective-permute-start(f32[24,8,256]{2,1,0:T(8,128)S(1)} %get-tuple-element.149), channel_id=1, source_target_pairs={{0,1},{1,0},{2,3},{3,2},{4,5},{5,4},{6,7},{7,6},{8,9},{9,8},{10,11... | collective-permute-start | bytes 589832 | tf_op jit(solution)/shard_map/ppermute | solution.py:405
  21.9 1.1 %collective-permute-done.3.refs_1_ = f32[24,8,256]{2,1,0:T(8,128)S(1)} collective-permute-done((f32[24,8,256]{2,1,0:T(8,128)S(1)}, f32[24,8,256]{2,1,0:T(8,128)S(1)}, u32[]{:S(2)}, u32[]{:S(2)}) %collective-permute-start.3) | collective-permute-done | bytes 196640 | tf_op jit(solution)/shard_map/ppermute | solution.py:405
  23.4 3.0 %collective-permute-done.2.refs_1_.refs_3_ = f32[312,256]{1,0:T(8,128)S(1)} collective-permute-done((f32[312,256]{1,0:T(8,128)S(1)}, f32[312,256]{1,0:T(8,128)S(1)}, u32[]{:S(2)}, u32[]{:S(2)}) %collective-permute-start.2) | collective-permute-done | bytes 319520 | tf_op jit(solution)/shard_map/ppermute | solution.py:405
  27.0 2.0 %collective-permute-start.4 = (f32[24,8,256]{2,1,0:T(8,128)S(1)}, f32[24,8,256]{2,1,0:T(8,128)S(1)}, u32[]{:S(2)}, u32[]{:S(2)}) collective-permute-start(f32[24,8,256]{2,1,0:T(8,128)S(1)} %get-tuple-element.159), channel_id=1, source_target_pairs={{0,1},{1,0},{2,3},{3,2},{4,5},{5,4},{6,7},{7,6},{8,9},{9,8},{10,11... | collective-permute-start | bytes 589832 | tf_op jit(solution)/shard_map/ppermute | solution.py:405
  29.0 1.1 %collective-permute-done.4.refs_1_ = f32[24,8,256]{2,1,0:T(8,128)S(1)} collective-permute-done((f32[24,8,256]{2,1,0:T(8,128)S(1)}, f32[24,8,256]{2,1,0:T(8,128)S(1)}, u32[]{:S(2)}, u32[]{:S(2)}) %collective-permute-start.4) | collective-permute-done | bytes 196640 | tf_op jit(solution)/shard_map/ppermute | solution.py:405
  30.1 0.9 %shard_map.162 = (f32[2,3,4,40,256]{4,3,2,1,0:T(8,128)S(1)}, f32[2,3,4,40,256]{4,3,2,1,0:T(8,128)S(1)}, f32[2,3,4,40,256]{4,3,2,1,0:T(8,128)S(1)}, f32[2,3,4,40,...) custom-call(f32[4,8,256]{2,1,0:T(8,128)S(1)} %get-tuple-element.125., ...), custom_call_target="tpu_custom_call", output_to_operand_aliasing={{0}: (2, {}), {1}: (3, {}), {2}: (4, {}), {3}: (5, {}), {6}... | custom-call | tf_op jit(solution)/shard_map/pallas_call | solution.py:390
  30.9 4.3 %collective-permute-start.5 = (f32[272,256]{1,0:T(8,128)S(1)}, f32[272,256]{1,0:T(8,128)S(1)}, u32[]{:S(2)}, u32[]{:S(2)}) collective-permute-start(f32[272,256]{1,0:T(8,128)S(1)} %get-tuple-element.165), channel_id=1, source_target_pairs={{2,4},{4,2},{6,8},{8,6},{10,12},{12,10},{14,0},{0,14},{3,5},{5,3},... | collective-permute-start | bytes 835592 | tf_op jit(solution)/shard_map/ppermute | solution.py:405
  36.6 1.1 %collective-permute-done.7.refs_1_ = f32[24,8,256]{2,1,0:T(8,128)S(1)} collective-permute-done((f32[24,8,256]{2,1,0:T(8,128)S(1)}, f32[24,8,256]{2,1,0:T(8,128)S(1)}, u32[]{:S(2)}, u32[]{:S(2)}) %collective-permute-start.7) | collective-permute-done | bytes 196640 | tf_op jit(solution)/shard_map/ppermute | solution.py:405
  38.1 3.7 %collective-permute-done.5.refs_1_ = f32[272,256]{1,0:T(8,128)S(1)} collective-permute-done((f32[272,256]{1,0:T(8,128)S(1)}, f32[272,256]{1,0:T(8,128)S(1)}, u32[]{:S(2)}, u32[]{:S(2)}) %collective-permute-start.5) | collective-permute-done | bytes 278560 | tf_op jit(solution)/shard_map/ppermute | solution.py:405
  42.4 1.2 %collective-permute-start.8 = (f32[24,8,256]{2,1,0:T(8,128)S(1)}, f32[24,8,256]{2,1,0:T(8,128)S(1)}, u32[]{:S(2)}, u32[]{:S(2)}) collective-permute-start(f32[24,8,256]{2,1,0:T(8,128)S(1)} %get-tuple-element.184), channel_id=1, source_target_pairs={{0,1},{1,0},{2,3},{3,2},{4,5},{5,4},{6,7},{7,6},{8,9},{9,8},{10,11... | collective-permute-start | bytes 589832 | tf_op jit(solution)/shard_map/ppermute | solution.py:405
  43.6 1.1 %collective-permute-done.8.refs_1_ = f32[24,8,256]{2,1,0:T(8,128)S(1)} collective-permute-done((f32[24,8,256]{2,1,0:T(8,128)S(1)}, f32[24,8,256]{2,1,0:T(8,128)S(1)}, u32[]{:S(2)}, u32[]{:S(2)}) %collective-permute-start.8) | collective-permute-done | bytes 196640 | tf_op jit(solution)/shard_map/ppermute | solution.py:405
  45.6 4.3 %collective-permute-start.9 = (f32[272,256]{1,0:T(8,128)S(1)}, f32[272,256]{1,0:T(8,128)S(1)}, u32[]{:S(2)}, u32[]{:S(2)}) collective-permute-start(f32[272,256]{1,0:T(8,128)S(1)} %get-tuple-element.190), channel_id=1, source_target_pairs={{2,4},{4,2},{6,8},{8,6},{10,12},{12,10},{14,0},{0,14},{3,5},{5,3},... | collective-permute-start | bytes 835592 | tf_op jit(solution)/shard_map/ppermute | solution.py:405
  51.2 1.1 %collective-permute-done.11.refs_1_ = f32[24,8,256]{2,1,0:T(8,128)S(1)} collective-permute-done((f32[24,8,256]{2,1,0:T(8,128)S(1)}, f32[24,8,256]{2,1,0:T(8,128)S(1)}, u32[]{:S(2)}, u32[]{:S(2)}) %collective-permute-start.11) | collective-permute-done | bytes 196640 | tf_op jit(solution)/shard_map/ppermute | solution.py:405
  52.7 3.8 %collective-permute-done.9.refs_1_ = f32[272,256]{1,0:T(8,128)S(1)} collective-permute-done((f32[272,256]{1,0:T(8,128)S(1)}, f32[272,256]{1,0:T(8,128)S(1)}, u32[]{:S(2)}, u32[]{:S(2)}) %collective-permute-start.9) | collective-permute-done | bytes 278560 | tf_op jit(solution)/shard_map/ppermute | solution.py:405
  57.0 1.1 %collective-permute-start.12 = (f32[24,8,256]{2,1,0:T(8,128)S(1)}, f32[24,8,256]{2,1,0:T(8,128)S(1)}, u32[]{:S(2)}, u32[]{:S(2)}) collective-permute-start(f32[24,8,256]{2,1,0:T(8,128)S(1)} %get-tuple-element.209), channel_id=1, source_target_pairs={{0,1},{1,0},{2,3},{3,2},{4,5},{5,4},{6,7},{7,6},{8,9},{9,8},{10,11... | collective-permute-start | bytes 589832 | tf_op jit(solution)/shard_map/ppermute | solution.py:405
  58.2 1.1 %collective-permute-done.12.refs_1_ = f32[24,8,256]{2,1,0:T(8,128)S(1)} collective-permute-done((f32[24,8,256]{2,1,0:T(8,128)S(1)}, f32[24,8,256]{2,1,0:T(8,128)S(1)}, u32[]{:S(2)}, u32[]{:S(2)}) %collective-permute-start.12) | collective-permute-done | bytes 196640 | tf_op jit(solution)/shard_map/ppermute | solution.py:405
  59.6 4.3 %collective-permute-start.13 = (f32[272,256]{1,0:T(8,128)S(1)}, f32[272,256]{1,0:T(8,128)S(1)}, u32[]{:S(2)}, u32[]{:S(2)}) collective-permute-start(f32[272,256]{1,0:T(8,128)S(1)} %get-tuple-element.215), channel_id=1, source_target_pairs={{2,4},{4,2},{6,8},{8,6},{10,12},{12,10},{14,0},{0,14},{3,5},{5,3},... | collective-permute-start | bytes 835592 | tf_op jit(solution)/shard_map/ppermute | solution.py:405
  64.5 7.9 %collective-permute-done.14.refs_1_ = f32[272,256]{1,0:T(8,128)S(1)} collective-permute-done((f32[272,256]{1,0:T(8,128)S(1)}, f32[272,256]{1,0:T(8,128)S(1)}, u32[]{:S(2)}, u32[]{:S(2)}) %collective-permute-start.14) | collective-permute-done | bytes 278560 | tf_op jit(solution)/shard_map/ppermute | solution.py:405
  74.8 1.7 %shard_map.174 = (f32[2,3,4,32,256]{4,3,2,1,0:T(8,128)}, f32[2,3,4,32,256]{4,3,2,1,0:T(8,128)}, f32[2,3,4,32,256]{4,3,2,1,0:T(8,128)}, f32[2,3,4,32,256]{4,3,2,1,0:T(8,128)}) custom-call(f32[2,3,4,40,256]{4,3,2,1,0:T(8,128)S(1)} %get-tuple-element.234.e, f32[2,3,4,40,256]{4,3,2,1,0:T(8,128)S(1)} %get-tuple-element.235.h, ...), custom_call_target="tpu_custom_call" | custom-call | flops 4194304 | bytes 4194304 | tf_op jit(solution)/shard_map/pallas_call | solution.py:390
  (44 shorter events, 13.8 us)
Async XLA Ops:
  2.6 0.7 copy-start.4
  2.6 0.7 copy-start.5
  2.6 0.7 copy-start.6
  2.6 0.7 copy-start.1
  2.7 0.7 copy-start.2
  2.7 0.7 copy-start.3
  2.7 1.8 %collective-permute-start = (f32[52,8,256]{2,1,0:T(8,128)S(1)}, f32[52,8,256]{2,1,0:T(8,128)S(1)}, u32[]{:S(2)}, u32[]{:S(2)}) collective-permute-start(f32[52,8,256]{2,1,0:T(8,128)S(1)} %get-tuple-element.126), channel_id=1, source_target_pairs={{0,1},{1,0},{2,3},{3,2},{4,5},{5,4},{6,7},{7,6},{8,9},{9,8},{10,11... | collective-permute-start | bytes 1277960 | tf_op jit(solution)/shard_map/ppermute | solution.py:405
  5.6 9.9 %collective-permute-start.1 = (f32[312,256]{1,0:T(8,128)S(1)}, f32[312,256]{1,0:T(8,128)S(1)}, u32[]{:S(2)}, u32[]{:S(2)}) collective-permute-start(f32[312,256]{1,0:T(8,128)S(1)} %get-tuple-element.139), channel_id=1, source_target_pairs={{0,2},{2,0},{4,6},{6,4},{8,10},{10,8},{12,14},{14,12},{1,3},{3,1},... | collective-permute-start | bytes 958472 | tf_op jit(solution)/shard_map/ppermute | solution.py:405
  15.6 10.8 %collective-permute-start.2 = (f32[312,256]{1,0:T(8,128)S(1)}, f32[312,256]{1,0:T(8,128)S(1)}, u32[]{:S(2)}, u32[]{:S(2)}) collective-permute-start(f32[312,256]{1,0:T(8,128)S(1)} %get-tuple-element.140), channel_id=1, source_target_pairs={{2,4},{4,2},{6,8},{8,6},{10,12},{12,10},{14,0},{0,14},{3,5},{5,3},... | collective-permute-start | bytes 958472 | tf_op jit(solution)/shard_map/ppermute | solution.py:405
  20.3 2.6 %collective-permute-start.3 = (f32[24,8,256]{2,1,0:T(8,128)S(1)}, f32[24,8,256]{2,1,0:T(8,128)S(1)}, u32[]{:S(2)}, u32[]{:S(2)}) collective-permute-start(f32[24,8,256]{2,1,0:T(8,128)S(1)} %get-tuple-element.149), channel_id=1, source_target_pairs={{0,1},{1,0},{2,3},{3,2},{4,5},{5,4},{6,7},{7,6},{8,9},{9,8},{10,11... | collective-permute-start | bytes 589832 | tf_op jit(solution)/shard_map/ppermute | solution.py:405
  23.3 11.9 %collective-permute-start.6 = (f32[272,256]{1,0:T(8,128)S(1)}, f32[272,256]{1,0:T(8,128)S(1)}, u32[]{:S(2)}, u32[]{:S(2)}) collective-permute-start(f32[272,256]{1,0:T(8,128)S(1)} %get-tuple-element.167), channel_id=1, source_target_pairs={{0,2},{2,0},{4,6},{6,4},{8,10},{10,8},{12,14},{14,12},{1,3},{3,1},... | collective-permute-start | bytes 835592 | tf_op jit(solution)/shard_map/ppermute | solution.py:405
  27.0 3.1 %collective-permute-start.4 = (f32[24,8,256]{2,1,0:T(8,128)S(1)}, f32[24,8,256]{2,1,0:T(8,128)S(1)}, u32[]{:S(2)}, u32[]{:S(2)}) collective-permute-start(f32[24,8,256]{2,1,0:T(8,128)S(1)} %get-tuple-element.159), channel_id=1, source_target_pairs={{0,1},{1,0},{2,3},{3,2},{4,5},{5,4},{6,7},{7,6},{8,9},{9,8},{10,11... | collective-permute-start | bytes 589832 | tf_op jit(solution)/shard_map/ppermute | solution.py:405
  30.9 10.9 %collective-permute-start.5 = (f32[272,256]{1,0:T(8,128)S(1)}, f32[272,256]{1,0:T(8,128)S(1)}, u32[]{:S(2)}, u32[]{:S(2)}) collective-permute-start(f32[272,256]{1,0:T(8,128)S(1)} %get-tuple-element.165), channel_id=1, source_target_pairs={{2,4},{4,2},{6,8},{8,6},{10,12},{12,10},{14,0},{0,14},{3,5},{5,3},... | collective-permute-start | bytes 835592 | tf_op jit(solution)/shard_map/ppermute | solution.py:405
  35.9 1.8 %collective-permute-start.7 = (f32[24,8,256]{2,1,0:T(8,128)S(1)}, f32[24,8,256]{2,1,0:T(8,128)S(1)}, u32[]{:S(2)}, u32[]{:S(2)}) collective-permute-start(f32[24,8,256]{2,1,0:T(8,128)S(1)} %get-tuple-element.174), channel_id=1, source_target_pairs={{0,1},{1,0},{2,3},{3,2},{4,5},{5,4},{6,7},{7,6},{8,9},{9,8},{10,11... | collective-permute-start | bytes 589832 | tf_op jit(solution)/shard_map/ppermute | solution.py:405
  38.1 11.9 %collective-permute-start.10 = (f32[272,256]{1,0:T(8,128)S(1)}, f32[272,256]{1,0:T(8,128)S(1)}, u32[]{:S(2)}, u32[]{:S(2)}) collective-permute-start(f32[272,256]{1,0:T(8,128)S(1)} %get-tuple-element.192), channel_id=1, source_target_pairs={{0,2},{2,0},{4,6},{6,4},{8,10},{10,8},{12,14},{14,12},{1,3},{3,1},... | collective-permute-start | bytes 835592 | tf_op jit(solution)/shard_map/ppermute | solution.py:405
  42.4 2.3 %collective-permute-start.8 = (f32[24,8,256]{2,1,0:T(8,128)S(1)}, f32[24,8,256]{2,1,0:T(8,128)S(1)}, u32[]{:S(2)}, u32[]{:S(2)}) collective-permute-start(f32[24,8,256]{2,1,0:T(8,128)S(1)} %get-tuple-element.184), channel_id=1, source_target_pairs={{0,1},{1,0},{2,3},{3,2},{4,5},{5,4},{6,7},{7,6},{8,9},{9,8},{10,11... | collective-permute-start | bytes 589832 | tf_op jit(solution)/shard_map/ppermute | solution.py:405
  45.6 10.9 %collective-permute-start.9 = (f32[272,256]{1,0:T(8,128)S(1)}, f32[272,256]{1,0:T(8,128)S(1)}, u32[]{:S(2)}, u32[]{:S(2)}) collective-permute-start(f32[272,256]{1,0:T(8,128)S(1)} %get-tuple-element.190), channel_id=1, source_target_pairs={{2,4},{4,2},{6,8},{8,6},{10,12},{12,10},{14,0},{0,14},{3,5},{5,3},... | collective-permute-start | bytes 835592 | tf_op jit(solution)/shard_map/ppermute | solution.py:405
  50.5 1.8 %collective-permute-start.11 = (f32[24,8,256]{2,1,0:T(8,128)S(1)}, f32[24,8,256]{2,1,0:T(8,128)S(1)}, u32[]{:S(2)}, u32[]{:S(2)}) collective-permute-start(f32[24,8,256]{2,1,0:T(8,128)S(1)} %get-tuple-element.199), channel_id=1, source_target_pairs={{0,1},{1,0},{2,3},{3,2},{4,5},{5,4},{6,7},{7,6},{8,9},{9,8},{10,11... | collective-permute-start | bytes 589832 | tf_op jit(solution)/shard_map/ppermute | solution.py:405
  57.0 2.2 %collective-permute-start.12 = (f32[24,8,256]{2,1,0:T(8,128)S(1)}, f32[24,8,256]{2,1,0:T(8,128)S(1)}, u32[]{:S(2)}, u32[]{:S(2)}) collective-permute-start(f32[24,8,256]{2,1,0:T(8,128)S(1)} %get-tuple-element.209), channel_id=1, source_target_pairs={{0,1},{1,0},{2,3},{3,2},{4,5},{5,4},{6,7},{7,6},{8,9},{9,8},{10,11... | collective-permute-start | bytes 589832 | tf_op jit(solution)/shard_map/ppermute | solution.py:405
  58.2 14.2 %collective-permute-start.14 = (f32[272,256]{1,0:T(8,128)S(1)}, f32[272,256]{1,0:T(8,128)S(1)}, u32[]{:S(2)}, u32[]{:S(2)}) collective-permute-start(f32[272,256]{1,0:T(8,128)S(1)} %get-tuple-element.217), channel_id=1, source_target_pairs={{0,2},{2,0},{4,6},{6,4},{8,10},{10,8},{12,14},{14,12},{1,3},{3,1},... | collective-permute-start | bytes 835592 | tf_op jit(solution)/shard_map/ppermute | solution.py:405
  59.6 13.4 %collective-permute-start.13 = (f32[272,256]{1,0:T(8,128)S(1)}, f32[272,256]{1,0:T(8,128)S(1)}, u32[]{:S(2)}, u32[]{:S(2)}) collective-permute-start(f32[272,256]{1,0:T(8,128)S(1)} %get-tuple-element.215), channel_id=1, source_target_pairs={{2,4},{4,2},{6,8},{8,6},{10,12},{12,10},{14,0},{0,14},{3,5},{5,3},... | collective-permute-start | bytes 835592 | tf_op jit(solution)/shard_map/ppermute | solution.py:405
  73.0 0.7 copy-start
  73.9 2.6 %collective-permute-start.15 = (f32[2,4,8,128]{3,2,1,0:T(8,128)S(1)}, f32[2,4,8,128]{3,2,1,0:T(8,128)S(1)}, u32[]{:S(2)}, u32[]{:S(2)}) collective-permute-start(f32[2,4,8,128]{3,2,1,0:T(8,128)S(1)} %shard_map.175.own), channel_id=1, source_target_pairs={{0,1},{1,0},{2,3},{3,2},{4,5},{5,4},{6,7},{7,6},{8,9},{9,8},{10,11... | collective-permute-start | bytes 98312 | tf_op jit(solution)/shard_map/ppermute | solution.py:405
